TPU v7x, 512 devices: a whole 4x8x8 slice. The times are simulated.
512 devices in a mesh: dp: 32 (over x, y), tp: 16 (over z, core).
Axes of the slice: x: 4, y: 8, z: 8, core: 2. Of those that a mesh axis runs over, the one named last changes fastest.
Arguments:
- embeddings: bfloat16 [12288, 192, 256], P(('dp', 'tp')), may hold values from -6 to 6
- projection: bfloat16 [256, 16], replicated, may hold values from -0.375 to 0.375
- compress: bfloat16 [256, 4], replicated, may hold values from -0.375 to 0.375
- w_up: bfloat16 [4096, 4096], P(None, 'tp'), may hold values from -0.09375 to 0.09375
- w_down: bfloat16 [4096, 768], P('tp'), may hold values from -0.125 to 0.125
- output_norm_gain: float32 [1536], P('tp'), may hold values from 0.25 to 1.75
- out_grad: bfloat16 [12288, 1536], P('dp', 'tp'), may hold values from -6 to 6
Outputs:
- block_result: bfloat16 [12288, 1536], P('dp', 'tp')
- grad_down: float32 [4096, 768], P(('tp', 'dp'))
All inputs are finite; a program needn't handle non-finite values.
Results may differ from a plain program's by a relative error of at most 0.017.
Values may be sent and summed in bfloat16 or wider, within the bound.
No kernel may reach another device: no remote copies, remote signals or barrier semaphores. Data moves between devices by JAX's collectives and lax.ppermute only.
A program may use at most 64 MiB of HBM per device.

v0:
```python
import jax
import jax.numpy as jnp
from jax import lax
from jax.sharding import PartitionSpec as P


def split_up(x, dim, devices):
    before, after = (x.shape[:dim], x.shape[dim + 1 :])
    return jnp.moveaxis(x.reshape(*before, devices, -1, *after), dim, 0)


def summed_on_arrival(x, axis, dim):
    parts = split_up(x, dim, lax.axis_size(axis))
    arrived = lax.all_to_all(parts, axis, split_axis=0, concat_axis=0, tiled=True)
    return arrived.astype(jnp.float32).sum(axis=0)


def sent_to_all(x, axis):
    devices = lax.axis_size(axis)
    return lax.all_to_all(jnp.broadcast_to(x[None], (devices, *x.shape)), axis, 0, 0, tiled=True)


def gathered_once(x, axis):
    leaves = jax.tree.leaves(x)
    sequence = sorted(range(len(leaves)), key=lambda k: -leaves[k].size)
    width = (1, *leaves[sequence[0]].shape)[-1]
    lines = [
        jnp.pad(leaves[k].reshape(-1), (0, -leaves[k].size % width)).reshape(-1, width)
        for k in sequence
    ]
    both, at, found = (sent_to_all(jnp.concatenate(lines), axis), 0, {})
    for k, line in zip(sequence, lines):
        share = both[:, at : at + len(line)].reshape(len(both), -1)
        found[k] = share[:, : leaves[k].size].reshape(-1, *leaves[k].shape)
        at += len(line)
    numbers = iter(range(len(leaves)))
    return jax.tree.map(lambda _: found[next(numbers)], x)


def joined_by_halves(pieces, combine):
    while len(jax.tree.leaves(pieces)[0]) > 1:
        pieces = jax.vmap(combine)(
            *(jax.tree.map(lambda part: part[side::2], pieces) for side in (0, 1))
        )
    return jax.tree.map(lambda part: part[0], pieces)


def joined_all(x, axis, combine):
    pieces = gathered_once(x, axis)
    return joined_by_halves(pieces, combine)


def turned_gather(arrays, axis, dims):
    turned = [jnp.moveaxis(a, dim, 0) for a, dim in zip(arrays, dims)]
    both = jnp.concatenate([t.reshape(len(t), -1) for t in turned], axis=1)
    filled, at, done = (lax.all_gather(both, axis, axis=0, tiled=True), 0, [])
    for t, dim in zip(turned, dims):
        share = filled[:, at : at + t[0].size].reshape(-1, *t.shape[1:])
        done.append(jnp.moveaxis(share, 0, dim))
        at += t[0].size
    return tuple(done)


def chan_merge(left, right):
    count_a, mean_a, dev_a = left
    count_b, mean_b, dev_b = right
    total = count_a + count_b
    delta = mean_b - mean_a
    row_average = mean_a + delta * (count_b / total)
    dev = dev_a + dev_b + delta * delta * (count_a * count_b / total)
    return (total, row_average, dev)


def on_device(embeddings, projection, compress, w_up, w_down, output_norm_gain, out_grad):
    samples = embeddings.shape[0]
    pairs = jnp.einsum(
        "sef,fk->sek", embeddings, projection, preferred_element_type=jnp.float32
    ).astype(jnp.bfloat16)
    inter = jnp.einsum(
        "sek,sef->skf", pairs, embeddings, preferred_element_type=jnp.float32
    ).reshape(samples, -1)
    center = inter - jnp.mean(inter, axis=1, keepdims=True)
    spread = jnp.mean(center * center, axis=1, keepdims=True)
    normed = (center / jnp.sqrt(spread + 1e-05)).astype(jnp.bfloat16)
    lcb = jnp.einsum(
        "sef,fj->sje", embeddings, compress, preferred_element_type=jnp.float32
    ).reshape(samples, -1)
    hidden = jax.nn.gelu(
        jnp.dot(
            lax.all_gather(normed, "tp", axis=0, tiled=True),
            w_up,
            preferred_element_type=jnp.float32,
        ),
        approximate=True,
    ).astype(jnp.bfloat16)
    group_rows = hidden.shape[0]
    tp_count = lax.axis_size("tp")
    mlp = jnp.dot(hidden, w_down, preferred_element_type=jnp.float32)
    mlp_width = mlp.shape[1]
    full_width = mlp_width + lcb.shape[1]
    width = full_width // tp_count
    mlp_share = summed_on_arrival(mlp.astype(jnp.bfloat16), "tp", 1)
    lcb_share = lax.all_to_all(
        lcb.astype(jnp.bfloat16), "tp", split_axis=1, concat_axis=0, tiled=True
    ).astype(lcb.dtype)
    mixed_rows = jnp.concatenate([mlp_share, lcb_share], axis=1)
    own_mean = jnp.mean(mixed_rows, axis=1)
    own_dev = jnp.sum((mixed_rows - own_mean[:, None]) ** 2, axis=1)
    own_count = jnp.full((), width, jnp.float32)
    total, row_average, dev = joined_all((own_count, own_mean, own_dev), "tp", chan_merge)
    inverse_deviation = 1.0 / jnp.sqrt(dev[:, None] / total + 1e-05)
    centered_rows = (mixed_rows - row_average[:, None]) * inverse_deviation
    block_result = (centered_rows * output_norm_gain).astype(jnp.bfloat16)
    scaled_rows = out_grad.astype(jnp.float32) * output_norm_gain
    entire_scaled_rows, entire_normalized_rows = tuple(
        (
            part.astype(jnp.float32)
            for part in turned_gather(
                (scaled_rows.astype(jnp.bfloat16), centered_rows.astype(jnp.bfloat16)), "tp", (1, 1)
            )
        )
    )
    first_moment = jnp.mean(entire_scaled_rows, axis=1, keepdims=True)
    second_moment = jnp.mean(entire_scaled_rows * entire_normalized_rows, axis=1, keepdims=True)
    mixed_gradient = (
        (entire_scaled_rows - first_moment - entire_normalized_rows * second_moment)
        * inverse_deviation
    ).astype(jnp.bfloat16)
    group_mlp = mlp_width // tp_count
    mlp_grad = mixed_gradient.reshape(group_rows, tp_count, -1)[:, :, :group_mlp].reshape(
        group_rows, -1
    )
    grad_down = summed_on_arrival(
        jnp.einsum("rh,rc->hc", hidden, mlp_grad, preferred_element_type=jnp.float32).astype(
            jnp.bfloat16
        ),
        "dp",
        0,
    )
    return (block_result, grad_down)


def solution(mesh):
    return jax.shard_map(
        on_device,
        mesh=mesh,
        in_specs=(
            P(("dp", "tp"), None, None),
            P(),
            P(),
            P(None, "tp"),
            P("tp", None),
            P("tp"),
            P("dp", "tp"),
        ),
        out_specs=(P("dp", "tp"), P(("tp", "dp"), None)),
        check_vma=False,
    )
```

profile of v0, /device:TPU:8, one launch (start us, length us, event | category | flops | bytes accessed | tf_op | source)
XLA Modules:
  0.0 184.7 jit_solution(13328559922858504637)
XLA Ops:
  7.2 0.0 copy-start
  7.2 0.0 copy-start.3
  7.2 0.0 all-gather.3.cloned.1.call-start
  7.2 1.6 copy-done
  8.8 1.8 fusion.26
  10.7 0.4 multiply_reduce_fusion
  11.1 0.2 copy.26
  11.3 0.8 divide_convert_fusion
  12.1 0.0 all-gather.3.cloned.1.call-update
  12.1 0.0 copy-done.3
  12.1 0.7 fusion.6
  12.9 0.1 convert_element_type.74
  13.0 0.8 reshape.145
  13.8 10.4 %all-to-all-start.1 = ((bf16[16,2,576]{2,1,0:T(2,128)(2,1)}), bf16[16,2,576]{2,1,0:T(2,128)(2,1)S(1)}, u32[]{:S(2)}, u32[]{:S(2)}) async-start(bf16[16,2,576]{2,1,0:T(2,128)(2,1)} %reshape.145), calls=%async_computation.1 | async-start | bytes 81920 | tf_op jit(solution)/shard_map/all_to_all | solution.py:103
  24.2 37.1 %all-gather.3.cloned.1.call-done = bf16[384,4096]{1,0:T(8,128)(2,1)} async-done(((bf16[24,4096]{1,0:T(8,128)(2,1)}), bf16[384,4096]{1,0:T(8,128)(2,1)}) %all-gather.3.cloned.1.call-update) | async-done | bytes 3145744 | tf_op jit(solution)/shard_map/all_gather | solution.py:90
  61.3 0.0 copy-start.6
  61.3 3.6 %fusion.29 = f32[384,256]{1,0:T(8,128)S(1)} fusion(bf16[384,4096]{1,0:T(8,128)(2,1)} %all-gather.3.cloned.1.call-done, bf16[4096,256]{1,0:T(8,128)(2,1)} %param.10), kind=kOutput, calls=%fused_computation.71 | convolution fusion | flops 805306368 | bytes 5636096 | tf_op jit(solution)/shard_map/dot_general | solution.py:89
  64.9 0.0 copy-start.7
  64.9 0.7 copy-done.7
  65.7 0.0 copy-done.6
  65.7 0.4 convolution_convert_fusion
  66.0 0.0 copy-start.4
  66.1 0.0 copy-start.2
  66.1 0.0 copy-start.5
  66.1 1.0 copy.19
  67.1 0.0 all-to-all-done.1
  67.1 4.3 %all-to-all-start = ((bf16[16,384,48]{1,2,0:T(8,128)(2,1)}), bf16[16,384,48]{1,2,0:T(8,128)(2,1)S(1)}, u32[]{:S(2)}, u32[]{:S(2)}) async-start(bf16[16,384,48]{1,2,0:T(8,128)(2,1)} %bitcast.2), calls=%async_computation | async-start | bytes 1179648 | tf_op jit(solution)/shard_map/all_to_all | solution.py:14
  71.4 0.0 all-gather.5.cloned.1.call-start
  71.5 0.1 reshape.146
  71.6 0.1 convert_reduce_fusion.4
  71.8 0.1 reduce_sum.108
  71.9 0.1 reduce_sum.110
  72.0 0.1 copy.21
  72.1 16.6 %all-to-all-done = bf16[16,384,48]{1,2,0:T(8,128)(2,1)S(1)} async-done(((bf16[16,384,48]{1,2,0:T(8,128)(2,1)}), bf16[16,384,48]{1,2,0:T(8,128)(2,1)S(1)}, u32[]{:S(2)}, u32[]{:S(2)}) %all-to-all-start) | async-done | bytes 589856 | tf_op jit(solution)/shard_map/all_to_all | solution.py:14
  88.7 0.2 convert_reduce_fusion.1
  88.9 0.0 copy-done.4
  89.0 12.5 %all_to_all.25 = f32[16,3,384]{2,1,0:T(4,128)S(1)} all-to-all(f32[16,3,384]{2,1,0:T(4,128)S(1)} %broadcast_in_dim.2), channel_id=1, replica_groups=mesh['dp'=32,'tp'=16] {'tp'}, dimensions={0} | all-to-all | bytes 147456 | tf_op jit(solution)/shard_map/all_to_all | solution.py:20
  101.5 0.1 fusion.24
  101.7 0.1 slice_reduce_fusion
  101.8 0.1 slice.104
  101.9 0.1 slice.105
  102.0 0.1 slice.108
  102.1 0.1 slice.109
  102.2 0.1 slice.112
  102.3 0.1 slice.113
  102.4 0.6 fusion.25
  105.6 0.1 multiply_add_fusion
  105.8 0.1 multiply_add_fusion.2
  106.6 0.1 multiply_add_fusion.4
  106.8 0.0 copy-done.2
  106.8 0.0 copy-done.5
  106.8 0.7 fusion.16
  107.5 0.7 pad_maximum_fusion.1
  108.2 0.0 all-gather.5.cloned.1.call-update
  108.2 40.1 %all-gather.5.cloned.1.call-done = bf16[1536,768]{1,0:T(8,128)(2,1)} async-done(((bf16[96,768]{1,0:T(8,128)(2,1)}), bf16[1536,768]{1,0:T(8,128)(2,1)}) %all-gather.5.cloned.1.call-update) | async-done | bytes 2359312 | tf_op jit(solution)/shard_map/all_gather | solution.py:56
  148.3 0.0 copy-start.1
  148.3 2.2 %convert_reduce_fusion = (f32[384]{0:T(512)S(1)}, f32[384]{0:T(512)S(1)}) fusion(bf16[1536,768]{1,0:T(8,128)(2,1)} %all-gather.5.cloned.1.call-done), kind=kLoop, calls=%fused_computation.2 | loop fusion | flops 2948352 | bytes 2362368 | tf_op jit(solution)/shard_map/reduce_sum | solution.py:123
  150.6 0.1 copy-done.1
  150.7 0.5 fusion.2
  151.2 0.1 slice.140
  151.3 0.4 copy-done.8
  151.7 0.5 fusion.4
  152.2 25.1 %all_to_all.26 = bf16[32,8,768]{2,1,0:T(8,128)(2,1)S(1)} all-to-all(bf16[32,8,768]{2,1,0:T(8,128)(2,1)S(1)} %fusion.4), channel_id=1, replica_groups=mesh['dp'=32,'tp'=16] {'dp'}, dimensions={0} | all-to-all | bytes 786432 | tf_op jit(solution)/shard_map/all_to_all | solution.py:14
  177.2 0.7 convert_reduce_fusion.3
  (34 shorter events, 0.5 us)
Async XLA Ops:
  7.2 1.7 copy-start
  7.2 5.0 %copy-start.3 = (bf16[256,4]{0,1:T(4,128)(2,1)S(1)}, bf16[256,4]{0,1:T(4,128)(2,1)}, u32[]{:S(2)}) copy-start(bf16[256,4]{0,1:T(4,128)(2,1)} %param.9) | copy-start | bytes 6148
  7.2 54.2 %all-gather.3.cloned.1.call-start = ((), (), s32[]{:S(2)}) async-start(), calls=%async_computation.4 | async-start | bytes 3342336 | tf_op jit(solution)/shard_map/all_gather | solution.py:90
  13.8 53.3 %all-to-all-start.1 = ((bf16[16,2,576]{2,1,0:T(2,128)(2,1)}), bf16[16,2,576]{2,1,0:T(2,128)(2,1)S(1)}, u32[]{:S(2)}, u32[]{:S(2)}) async-start(bf16[16,2,576]{2,1,0:T(2,128)(2,1)} %reshape.145), calls=%async_computation.1 | async-start | bytes 81920 | tf_op jit(solution)/shard_map/all_to_all | solution.py:103
  61.3 4.3 %copy-start.6 = (bf16[256,768]{1,0:T(8,128)(2,1)S(1)}, bf16[256,768]{1,0:T(8,128)(2,1)}, u32[]{:S(2)}) copy-start(bf16[256,768]{1,0:T(8,128)(2,1)} %param.11) | copy-start | bytes 1179652
  64.9 0.7 copy-start.7
  66.0 22.9 %copy-start.4 = (f32[1,384]{1,0:T(1,128)S(1)}, f32[1,384]{1,0:T(1,128)}, u32[]{:S(2)}) copy-start(f32[1,384]{1,0:T(1,128)} %constant.29.clone.1) | copy-start | bytes 4612
  66.1 40.7 %copy-start.2 = (bf16[384,96]{0,1:T(8,128)(2,1)S(1)}, bf16[384,96]{0,1:T(8,128)(2,1)}, u32[]{:S(2)}) copy-start(bf16[384,96]{0,1:T(8,128)(2,1)} %param.13) | copy-start | bytes 221188
  66.1 40.7 %copy-start.5 = (f32[96]{0:T(128)S(1)}, f32[96]{0:T(128)}, u32[]{:S(2)}) copy-start(f32[96]{0:T(128)} %param.12) | copy-start | bytes 1156
  67.1 21.5 %all-to-all-start = ((bf16[16,384,48]{1,2,0:T(8,128)(2,1)}), bf16[16,384,48]{1,2,0:T(8,128)(2,1)S(1)}, u32[]{:S(2)}, u32[]{:S(2)}) async-start(bf16[16,384,48]{1,2,0:T(8,128)(2,1)} %bitcast.2), calls=%async_computation | async-start | bytes 1179648 | tf_op jit(solution)/shard_map/all_to_all | solution.py:14
  71.4 76.9 %all-gather.5.cloned.1.call-start = ((), (), s32[]{:S(2)}) async-start(), calls=%async_computation.5 | async-start | bytes 2506752 | tf_op jit(solution)/shard_map/all_gather | solution.py:56
  148.3 2.4 %copy-start.1 = (bf16[1536,768]{1,0:T(8,128)(2,1)S(1)}, bf16[1536,768]{1,0:T(8,128)(2,1)}, u32[]{:S(2)}) copy-start(bf16[1536,768]{1,0:T(8,128)(2,1)} %all-gather.5.cloned.1.call-done) | copy-start | bytes 7077892
  150.7 1.0 copy-start.8
Sparse Core Ops, SparseCore 0:
  12.3 49.0 all-gather.2
  108.3 39.9 all-gather.4
where the time goes:
time: 185 us
  waiting for transfers between devices  93.8 us (51%)
  blocking collectives  37.6 us (20%)
  between operations  17.6 us (10%)
  starting transfers between devices  14.8 us (8%)
  local copies, waits for them, and re-layouts  7.2 us (4%)
  matrix products  6.93 us (4%)
  other arithmetic  6.77 us (4%)
    all_gather x1, waiting for transfers between devices, turned_gather(): filled, at, done = (lax.all_gather(both, axis, axis=0, tiled=True), 0, [])  40.1 us
    all_gather x1, waiting for transfers between devices, on_device(): lax.all_gather(normed, 'tp', axis=0, tiled=True)  37.1 us
    all_to_all x1, blocking collectives, summed_on_arrival(): lax.all_to_all(parts, axis, split_axis=0, concat_axis=0, tiled=True)  25.1 us
    all_to_all x1, waiting for transfers between devices, summed_on_arrival(): lax.all_to_all(parts, axis, split_axis=0, concat_axis=0, tiled=True)  16.6 us
    all_to_all x1, blocking collectives, sent_to_all(): lax.all_to_all(jnp.broadcast_to(x[None], (devices, *x.shape)), axis, 0, 0...  12.5 us
    all_to_all x1, starting transfers between devices, on_device(): lax.all_to_all(lcb.astype(jnp.bfloat16), 'tp', split_axis=1, concat_axis=...  10.4 us
    all_to_all x1, starting transfers between devices, summed_on_arrival(): lax.all_to_all(parts, axis, split_axis=0, concat_axis=0, tiled=True)  4.3 us
    unnamed x22, local copies, waits for them, and re-layouts  4.06 us
  transfers between devices with their start and end apart: 4, of which 3 were waited for; matrix products, arithmetic and copies ran while one was open for 4% of the time, Pallas kernels for 0%

commit v1 on v0

v1 whole, which is shorter than its diff:
```python
import jax
import jax.numpy as jnp
from jax import lax
from jax.sharding import PartitionSpec as P

BF16, F16, F32 = jnp.bfloat16, jnp.float16, jnp.float32
NORMED_SCALE, LCB_SCALE, GG_SCALE = 512.0, 64.0, 4096.0


def high_low(x):
    high = lax.reduce_precision(x, 8, 7)
    return high.astype(BF16), (x - high).astype(BF16)


def on_device(embeddings, projection, compress, w_up, w_down, output_norm_gain, out_grad):
    samples, edim, fields = embeddings.shape
    tp = lax.axis_size("tp")
    dp = lax.axis_size("dp")
    me = lax.axis_index("tp")
    core = me % 2
    group_rows = samples * tp
    feat, fmw = w_up.shape[0], w_down.shape[1]
    own = fmw // tp
    width = 2 * own

    pairs = jnp.einsum("sef,fk->sek", embeddings, projection, preferred_element_type=F32).astype(BF16)
    inter = jnp.einsum("sek,sef->skf", pairs, embeddings, preferred_element_type=F32).reshape(samples, -1)
    center = inter - jnp.mean(inter, axis=1, keepdims=True)
    spread = jnp.mean(center * center, axis=1, keepdims=True)
    normed = (center * (NORMED_SCALE / jnp.sqrt(spread + 1e-05))).astype(F16)
    lcb = jnp.einsum("sef,fj->sje", embeddings, compress, preferred_element_type=F32).reshape(samples, -1)

    gg = out_grad.T.astype(F32) * output_norm_gain[:, None]
    gg_packed = (
        (gg[:own] * GG_SCALE).astype(F16).reshape(3, 2, 8, group_rows).transpose(0, 2, 1, 3).reshape(samples, -1)
    )
    sent = jnp.concatenate([normed, (lcb * LCB_SCALE).astype(F16), gg_packed], axis=1)
    got = lax.all_gather(sent, "tp", axis=0, tiled=True)

    pre = jnp.dot(got[:, :feat].astype(BF16), w_up, preferred_element_type=F32)
    hidden = jax.nn.gelu(pre * (1.0 / NORMED_SCALE), approximate=True).astype(BF16)
    mlp = jnp.einsum("hc,sh->cs", w_down, hidden, preferred_element_type=F32)
    mlp = mlp.reshape(tp // 2, 2, own, group_rows)

    swap = [(i, i ^ 1) for i in range(tp)]
    theirs = lax.dynamic_index_in_dim(mlp, 1 - core, 1, keepdims=False).astype(BF16)
    mine = lax.dynamic_index_in_dim(mlp, core, 1, keepdims=False)
    chip_sum = (mine + lax.ppermute(theirs, "tp", swap).astype(F32)).astype(BF16)
    same_core = [list(range(c, tp, 2)) for c in range(2)]
    arrived = lax.all_to_all(chip_sum, "tp", 0, 0, tiled=True, axis_index_groups=same_core)
    mlp_own = arrived.astype(F32).sum(axis=0)

    lcb_own = lax.dynamic_slice_in_dim(got[:, feat : feat + fmw], me * own, own, 1)
    lcb_own = lcb_own.astype(F32).T * (1.0 / LCB_SCALE)
    mix = jnp.concatenate([mlp_own, lcb_own], axis=0)

    own_mean = jnp.mean(mix, axis=0)
    delta = mix - own_mean
    own_dev = jnp.sum(delta * delta, axis=0)
    own_g = jnp.sum(gg, axis=0)
    own_gd = jnp.sum(gg * delta, axis=0)
    stats = jnp.stack([own_mean, own_dev, own_g, own_gd])
    message = jnp.concatenate([delta[:own].astype(BF16), *high_low(stats)], axis=0)
    every = lax.all_gather(message, "tp", axis=0, tiled=False)

    numbers = every[:, own : own + 4].astype(F32) + every[:, own + 4 :].astype(F32)
    means, devs, gs, gds = (numbers[:, k] for k in range(4))
    full = width * tp
    mean = jnp.mean(means, axis=0)
    shift = means - mean
    var = (jnp.sum(devs, axis=0) + width * jnp.sum(shift * shift, axis=0)) / full
    rstd = 1.0 / jnp.sqrt(var + 1e-05)
    first = jnp.sum(gs, axis=0) / full
    second = jnp.sum(gds + shift * gs, axis=0) * rstd / full

    block = (delta + (own_mean - mean)) * rstd * output_norm_gain[:, None]
    block_result = block.astype(BF16).T

    gg_all = (
        got[:, feat + fmw :].reshape(tp, 3, 8, 2, group_rows).transpose(0, 1, 3, 2, 4).reshape(tp, own, group_rows)
    )
    xhat = (every[:, :own].astype(F32) + shift[:, None]) * rstd
    dmix = ((gg_all.astype(F32) * (1.0 / GG_SCALE) - first - xhat * second) * rstd).astype(BF16)
    dmix = dmix.reshape(fmw, group_rows)
    grad = jnp.einsum("sh,cs->hc", hidden, dmix, preferred_element_type=F32).astype(BF16)
    parts = lax.all_to_all(grad.reshape(dp, -1, fmw), "dp", 0, 0, tiled=True)
    return block_result, parts.astype(F32).sum(axis=0)


def solution(mesh):
    return jax.shard_map(
        on_device,
        mesh=mesh,
        in_specs=(
            P(("dp", "tp"), None, None),
            P(),
            P(),
            P(None, "tp"),
            P("tp", None),
            P("tp"),
            P("dp", "tp"),
        ),
        out_specs=(P("dp", "tp"), P(("tp", "dp"), None)),
        check_vma=False,
    )
```

time: 185 us -> 121 us (0.65)
  waiting for transfers between devices: 93.8 us -> 23.5 us
  blocking collectives: 37.6 us -> 55.3 us
  between operations: 17.6 us -> 0.93 us
  local copies, waits for them, and re-layouts: 7.2 us -> 10.6 us
  matrix products: 6.93 us -> 5.05 us
    all_gather x2 -> x0, waiting for transfers between devices: 77.2 us -> none  [the longest x1 40.1 us: turned_gather(): filled, at, done = (lax.all_gather(both, axis, axis=0, tiled=True), 0, [])]
    all_gather x0 -> x2, blocking collectives: none -> 55.3 us  [the longest x1 38.7 us: on_device(): got = lax.all_gather(sent, 'tp', axis=0, tiled=True)]
    all_to_all x2 -> x0, blocking collectives: 37.6 us -> none  [the longest x1 25.1 us: summed_on_arrival(): lax.all_to_all(parts, axis, split_axis=0, concat_axis=0, tiled=True)]
    all_to_all x2, waiting for transfers between devices: 16.6 us -> 22.4 us  [the longest x1 14.7 us: on_device(): parts = lax.all_to_all(grad.reshape(dp, -1, fmw), 'dp', 0, 0, tiled=True)]
    mul x0 -> x2, local copies, waits for them, and re-layouts: none -> 2.98 us  [on_device(): gg_all.astype(F32) * (1.0 / GG_SCALE) - first - xhat * second]
    ppermute x0 -> x1, starting transfers between devices: none -> 2.28 us  [on_device(): lax.ppermute(theirs, 'tp', swap).astype(F32)]
    dot_general x5, matrix products: 6.93 us -> 5.05 us  [the longest x1 1.42 us: on_device(): jnp.einsum('sef,fj->sje', embeddings, compress, preferred_element_type=F32)]
    unnamed x22 -> x26, local copies, waits for them, and re-layouts: 4.06 us -> 4.87 us
  transfers between devices with their start and end apart: 4 -> 3, of which waited for: 3 -> 3; matrix products, arithmetic and copies ran while one was open for 4% -> 5% of each run, Pallas kernels for 0% -> 0%
where the time goes in v1:
time: 121 us; the launch traced here: 120 us
  blocking collectives  55.3 us (46%)
  waiting for transfers between devices  23.5 us (19%)
  starting transfers between devices  16.5 us (14%)
  local copies, waits for them, and re-layouts  10.6 us (9%)
  other arithmetic  8.4 us (7%)
  matrix products  5.05 us (4%)
    all_gather x1, blocking collectives, on_device(): got = lax.all_gather(sent, 'tp', axis=0, tiled=True)  38.7 us
    all_gather x1, blocking collectives, on_device(): every = lax.all_gather(message, 'tp', axis=0, tiled=False)  16.6 us
    all_to_all x1, waiting for transfers between devices, on_device(): parts = lax.all_to_all(grad.reshape(dp, -1, fmw), 'dp', 0, 0, tiled=True)  14.7 us
    all_to_all x1, starting transfers between devices, on_device(): parts = lax.all_to_all(grad.reshape(dp, -1, fmw), 'dp', 0, 0, tiled=True)  10.2 us
    all_to_all x1, waiting for transfers between devices, on_device(): lax.all_to_all(chip_sum, 'tp', 0, 0, tiled=True, axis_index_groups=same_c...  7.68 us
    unnamed x26, local copies, waits for them, and re-layouts  4.87 us
    all_to_all x1, starting transfers between devices, on_device(): lax.all_to_all(chip_sum, 'tp', 0, 0, tiled=True, axis_index_groups=same_c...  4.06 us
    mul x2, local copies, waits for them, and re-layouts, on_device(): gg_all.astype(F32) * (1.0 / GG_SCALE) - first - xhat * second  2.98 us
  transfers between devices with their start and end apart: 3, of which 3 were waited for; matrix products, arithmetic and copies ran while one was open for 5% of the time, Pallas kernels for 0%

profile of v1, /device:TPU:8, one launch (start us, length us, event | category | flops | bytes accessed | tf_op | source)
XLA Modules:
  0.0 120.3 jit_solution(396855091383316326)
XLA Ops:
  0.6 0.0 copy-start
  0.7 1.6 %copy-done = bf16[24,192,256]{2,1,0:T(8,128)(2,1)S(1)} copy-done((bf16[24,192,256]{2,1,0:T(8,128)(2,1)S(1)}, bf16[24,192,256]{2,1,0:T(8,128)(2,1)}, u32[]{:S(2)}) %copy-start) | copy-done | bytes 2359320
  2.3 0.0 copy-start.7
  2.3 0.0 copy-start.10
  2.3 0.0 copy-start.9
  2.3 1.4 %fusion.8 = f16[24,4,192]{2,1,0:T(4,128)(2,1)S(1)} fusion(bf16[24,192,256]{2,1,0:T(8,128)(2,1)S(1)} %copy-done, bf16[256,4]{0,1:T(4,128)(2,1)} %param.9), kind=kOutput, calls=%fused_computation.15 | convolution fusion | flops 9474048 | bytes 2398208 | tf_op jit(solution)/shard_map/sef,fj->sje/dot_general | solution.py:31
  3.7 0.1 convert_element_type.84
  3.9 0.0 copy-done.7
  3.9 0.0 copy-done.10
  3.9 0.1 fusion.19
  4.0 0.0 copy-done.9
  4.0 1.1 fusion.33
  5.1 0.4 multiply_reduce_fusion
  5.5 0.2 copy.52
  5.8 0.1 multiply_convert_fusion
  5.9 0.1 pad_maximum_fusion
  6.0 0.0 copy-start.11
  6.0 38.7 %all-gather.2 = f16[384,5632]{1,0:T(8,128)(2,1)S(1)} all-gather(f16[24,5632]{1,0:T(8,128)(2,1)S(1)} %pad_maximum_fusion), channel_id=1, replica_groups=mesh['dp'=32,'tp'=16] {'tp'}, dimensions={0}, use_global_device_ids=true | all-gather | bytes 4595712 | tf_op jit(solution)/shard_map/all_gather | solution.py:38
  44.7 0.0 copy-done.11
  44.7 0.0 copy-start.1
  44.7 0.0 copy-start.6
  44.7 1.0 fusion.17
  45.8 0.9 copy-done.1
  46.7 0.0 copy-start.2
  46.7 0.7 copy-done.2
  47.4 0.0 copy-done.6
  47.4 0.3 convolution_bitcast_fusion
  47.7 1.4 %copy.40 = f32[768,384]{1,0:T(8,128)} copy(f32[768,384]{0,1:T(8,128)S(1)} %convolution_bitcast_fusion) | data formatting | bytes 2359296 | tf_op jit(solution)/shard_map/hc,sh->cs/dot_general | solution.py:42
  49.1 1.1 fusion.18
  50.2 2.3 %collective-permute-start = (bf16[8,48,384]{2,1,0:T(8,128)(2,1)S(1)}, bf16[8,48,384]{2,1,0:T(8,128)(2,1)S(1)}, u32[]{:S(2)}, u32[]{:S(2)}) collective-permute-start(bf16[8,48,384]{2,1,0:T(8,128)(2,1)S(1)} %fusion.18), channel_id=1, source_target_pairs={{0,1},{1,0},{2,3},{3,2},{4,5},{5,4},{6,7},{7,6},{8,9},{9,8},{10,11... | collective-permute-start | bytes 884744 | tf_op jit(solution)/shard_map/ppermute | solution.py:48
  52.5 0.0 slice-start
  52.5 1.2 collective-permute-done
  53.7 1.9 %fusion.9 = bf16[8,48,384]{2,1,0:T(8,128)(2,1)} fusion(bf16[8,48,384]{2,1,0:T(8,128)(2,1)S(1)} %collective-permute-done, f32[8,2,48,384]{3,2,1,0:T(8,128)} %bitcast.76, s32[]{:T(128)S(6)} %select_n.18), kind=kLoop, calls=%fused_computation.21 | loop fusion | flops 442368 | bytes 1179652 | tf_op jit(solution)/shard_map/convert_element_type | solution.py:48
  55.5 4.1 %all-to-all-start = ((bf16[8,48,384]{2,1,0:T(8,128)(2,1)}), bf16[8,48,384]{2,1,0:T(8,128)(2,1)}, u32[]{:S(2)}, u32[]{:S(2)}) async-start(bf16[8,48,384]{2,1,0:T(8,128)(2,1)} %fusion.9), calls=%async_computation | async-start | bytes 589824 | tf_op jit(solution)/shard_map/all_to_all | solution.py:50
  59.6 0.0 slice-done
  59.6 0.1 constant_dynamic-slice_fusion
  59.8 0.7 copy.47
  60.5 1.2 convert_multiply_fusion
  61.7 1.6 %mul.195 = f32[16,3,8,2,384]{4,3,2,1,0:T(2,128)} reshape(f32[384,768]{1,0:T(8,128)S(1)} %convert_multiply_fusion) | data formatting | bytes 2359296 | tf_op jit(solution)/shard_map/mul | solution.py:83
  63.3 0.0 copy-start.8
  63.3 1.4 %copy.43 = f32[16,3,2,8,384]{4,3,2,1,0:T(8,128)S(1)} copy(f32[16,3,2,8,384]{4,2,3,1,0:T(2,128)} %bitcast.74) | data formatting | bytes 2359296 | tf_op jit(solution)/shard_map/mul | solution.py:83
  64.7 0.0 copy-done.8
  64.7 0.6 fusion.24
  65.3 7.7 %all-to-all-done = bf16[8,48,384]{2,1,0:T(8,128)(2,1)} async-done(((bf16[8,48,384]{2,1,0:T(8,128)(2,1)}), bf16[8,48,384]{2,1,0:T(8,128)(2,1)}, u32[]{:S(2)}, u32[]{:S(2)}) %all-to-all-start) | async-done | bytes 294944 | tf_op jit(solution)/shard_map/all_to_all | solution.py:50
  73.0 1.1 convert_reduce_fusion.1
  74.1 1.0 multiply_reduce_fusion.2
  75.1 0.0 copy-start.4
  75.2 16.6 %all-gather = bf16[896,384]{1,0:T(8,128)(2,1)S(1)} all-gather(bf16[56,384]{1,0:T(8,128)(2,1)S(1)} %pad_maximum_fusion.1), channel_id=2, replica_groups=mesh['dp'=32,'tp'=16] {'tp'}, dimensions={0}, use_global_device_ids=true | all-gather | bytes 731136 | tf_op jit(solution)/shard_map/all_gather | solution.py:64
  91.8 0.1 slice_reduce_fusion.1
  92.0 0.0 copy-done.4
  92.0 0.0 copy-start.3
  92.0 0.3 fusion.5
  92.3 0.0 copy-start.5
  92.3 0.6 copy-done.3
  92.9 1.1 fusion.1
  94.1 10.2 %all-to-all-start.1 = ((bf16[32,8,768]{2,1,0:T(8,128)(2,1)}), bf16[32,8,768]{2,1,0:T(8,128)(2,1)S(1)}, u32[]{:S(2)}, u32[]{:S(2)}) async-start(bf16[32,8,768]{2,1,0:T(8,128)(2,1)} %fusion.1), calls=%async_computation.1 | async-start | bytes 786432 | tf_op jit(solution)/shard_map/all_to_all | solution.py:86
  104.2 0.0 copy-done.5
  104.3 0.7 fusion.21
  105.0 14.7 %all-to-all-done.1 = bf16[32,8,768]{2,1,0:T(8,128)(2,1)S(1)} async-done(((bf16[32,8,768]{2,1,0:T(8,128)(2,1)}), bf16[32,8,768]{2,1,0:T(8,128)(2,1)S(1)}, u32[]{:S(2)}, u32[]{:S(2)}) %all-to-all-start.1) | async-done | bytes 393248 | tf_op jit(solution)/shard_map/all_to_all | solution.py:86
  119.7 0.7 convert_reduce_fusion
  (16 shorter events, 0.2 us)
Async XLA Ops:
  0.6 1.7 %copy-start = (bf16[24,192,256]{2,1,0:T(8,128)(2,1)S(1)}, bf16[24,192,256]{2,1,0:T(8,128)(2,1)}, u32[]{:S(2)}) copy-start(bf16[24,192,256]{2,1,0:T(8,128)(2,1)} %param.7) | copy-start | bytes 7077892
  2.3 1.6 %copy-start.7 = (bf16[384,96]{0,1:T(8,128)(2,1)S(1)}, bf16[384,96]{0,1:T(8,128)(2,1)}, u32[]{:S(2)}) copy-start(bf16[384,96]{0,1:T(8,128)(2,1)} %param.13) | copy-start | bytes 221188
  2.3 1.6 %copy-start.10 = (f32[96]{0:T(128)S(1)}, f32[96]{0:T(128)}, u32[]{:S(2)}) copy-start(f32[96]{0:T(128)} %param.12) | copy-start | bytes 1156
  2.3 1.7 %copy-start.9 = (bf16[256,16]{0,1:T(8,128)(2,1)S(1)}, bf16[256,16]{0,1:T(8,128)(2,1)}, u32[]{:S(2)}) copy-start(bf16[256,16]{0,1:T(8,128)(2,1)} %param.8) | copy-start | bytes 24580
  6.0 38.7 %copy-start.11 = (bf16[4096,256]{1,0:T(8,128)(2,1)S(1)}, bf16[4096,256]{1,0:T(8,128)(2,1)}, u32[]{:S(2)}) copy-start(bf16[4096,256]{1,0:T(8,128)(2,1)} %param.10) | copy-start | bytes 6291460
  44.7 2.0 %copy-start.1 = (f16[384,5632]{1,0:T(8,128)(2,1)}, f16[384,5632]{1,0:T(8,128)(2,1)S(1)}, u32[]{:S(2)}) copy-start(f16[384,5632]{1,0:T(8,128)(2,1)S(1)} %all-gather.2) | copy-start | bytes 12976132
  44.7 2.7 %copy-start.6 = (bf16[256,768]{1,0:T(8,128)(2,1)S(1)}, bf16[256,768]{1,0:T(8,128)(2,1)}, u32[]{:S(2)}) copy-start(bf16[256,768]{1,0:T(8,128)(2,1)} %param.11) | copy-start | bytes 1179652
  46.7 0.7 copy-start.2
  50.2 3.5 %collective-permute-start = (bf16[8,48,384]{2,1,0:T(8,128)(2,1)S(1)}, bf16[8,48,384]{2,1,0:T(8,128)(2,1)S(1)}, u32[]{:S(2)}, u32[]{:S(2)}) collective-permute-start(bf16[8,48,384]{2,1,0:T(8,128)(2,1)S(1)} %fusion.18), channel_id=1, source_target_pairs={{0,1},{1,0},{2,3},{3,2},{4,5},{5,4},{6,7},{7,6},{8,9},{9,8},{10,11... | collective-permute-start | bytes 884744 | tf_op jit(solution)/shard_map/ppermute | solution.py:48
  52.5 7.1 %slice-start = ((f16[384,5632]{1,0:T(8,128)(2,1)}), f16[384,768]{1,0:T(8,128)(2,1)S(1)}, s32[]{:S(2)}) async-start(f16[384,5632]{1,0:T(8,128)(2,1)} %copy-done.1), calls=%async_computation.2 | async-start | bytes 1179648 | tf_op jit(solution)/shard_map/slice | solution.py:53
  55.5 17.5 %all-to-all-start = ((bf16[8,48,384]{2,1,0:T(8,128)(2,1)}), bf16[8,48,384]{2,1,0:T(8,128)(2,1)}, u32[]{:S(2)}, u32[]{:S(2)}) async-start(bf16[8,48,384]{2,1,0:T(8,128)(2,1)} %fusion.9), calls=%async_computation | async-start | bytes 589824 | tf_op jit(solution)/shard_map/all_to_all | solution.py:50
  63.3 1.4 %copy-start.8 = (f16[384,48]{0,1:T(8,128)(2,1)S(1)}, f16[384,48]{0,1:T(8,128)(2,1)}, u32[]{:S(2)}) copy-start(f16[384,48]{0,1:T(8,128)(2,1)} %copy.47) | copy-start | bytes 110596
  75.1 16.9 %copy-start.4 = (f32[96,384]{1,0:T(8,128)}, f32[96,384]{1,0:T(8,128)S(1)}, u32[]{:S(2)}) copy-start(f32[96,384]{1,0:T(8,128)S(1)} %get-tuple-element.15) | copy-start | bytes 442372
  92.0 0.9 copy-start.3
  92.3 11.9 %copy-start.5 = (f32[96,384]{1,0:T(8,128)S(1)}, f32[96,384]{1,0:T(8,128)}, u32[]{:S(2)}) copy-start(f32[96,384]{1,0:T(8,128)} %copy-done.4) | copy-start | bytes 442372
  94.1 25.6 %all-to-all-start.1 = ((bf16[32,8,768]{2,1,0:T(8,128)(2,1)}), bf16[32,8,768]{2,1,0:T(8,128)(2,1)S(1)}, u32[]{:S(2)}, u32[]{:S(2)}) async-start(bf16[32,8,768]{2,1,0:T(8,128)(2,1)} %fusion.1), calls=%async_computation.1 | async-start | bytes 786432 | tf_op jit(solution)/shard_map/all_to_all | solution.py:86

commit v2 on v1

v2 whole, which is shorter than its diff:
```python
import jax
import jax.numpy as jnp
from jax import lax
from jax.experimental import pallas as pl
from jax.experimental.pallas import tpu as pltpu
from jax.sharding import PartitionSpec as P

BF16, F16, F32 = jnp.bfloat16, jnp.float16, jnp.float32
NORMED_SCALE, LCB_SCALE, GG_SCALE = 512.0, 64.0, 4096.0
NT = (((1,), (1,)), ((), ()))
MIB = 1 << 20


def call(kernel, out_shape, *operands, flops=0, nbytes=0, vmem=16, **kw):
    return pl.pallas_call(
        kernel,
        out_shape=out_shape,
        compiler_params=pltpu.CompilerParams(vmem_limit_bytes=vmem * MIB),
        cost_estimate=pl.CostEstimate(flops=flops, bytes_accessed=nbytes, transcendentals=0),
        **kw,
    )(*operands)


def column(gain):
    return jnp.broadcast_to(gain, (8, gain.shape[1])).T[:, :1]


def front_kernel(*refs):
    sources, refs = refs[:5], refs[5:]
    out_ref, gg_ref, x_ref, projection_ref, compress_ref, og_ref, gain_ref, inter, lcb, w, sent_ref, sems = refs
    samples, edim, fields = x_ref.shape
    steps, rank, block = inter.shape[:3]
    nl = lcb.shape[1]
    width, rows = gg_ref.shape
    own = width // 2
    copies = [
        pltpu.make_async_copy(source, target, sems.at[k])
        for k, (source, target) in enumerate(
            zip(sources[1:], (projection_ref, compress_ref, og_ref, gain_ref))
        )
    ]
    chunks = [
        pltpu.make_async_copy(
            sources[0].at[pl.ds(r * block, block)], x_ref.at[pl.ds(r * block, block)], sems.at[len(copies) + r]
        )
        for r in range(steps)
    ]
    for copy in copies[:2] + chunks + copies[2:]:
        copy.start()

    w[...] = jnp.zeros_like(w)
    copies[0].wait()
    copies[1].wait()
    w[:rank] = projection_ref[...].astype(F32)
    w[rank : rank + nl] = compress_ref[...].astype(F32)
    start = nl * edim + own * rows // samples
    for r in range(steps):
        chunks[r].wait()
        x = x_ref[r * block : (r + 1) * block]
        both = lax.dot_general(x.reshape(block * edim, fields), w[...].astype(BF16), NT, preferred_element_type=F32)
        for i in range(block):
            turned = both[i * edim : (i + 1) * edim].T
            lcb[r, :, i, :] = turned[rank : rank + nl]
            inter[r, :, i, :] = jnp.dot(turned[:rank].astype(BF16), x[i], preferred_element_type=F32)
        at = slice(r * block, (r + 1) * block)
        lines = [inter[r, k] for k in range(rank)]
        mean = jnp.sum(sum(lines[1:], lines[0]), axis=1, keepdims=True) / (rank * fields)
        lines = [line - mean for line in lines]
        squares = [line * line for line in lines]
        spread = jnp.sum(sum(squares[1:], squares[0]), axis=1, keepdims=True) / (rank * fields)
        factor = NORMED_SCALE / jnp.sqrt(spread + 1e-05)
        for k in range(rank):
            sent_ref[at, start + k * fields : start + (k + 1) * fields] = lines[k] * factor
        for j in range(nl):
            sent_ref[at, j * edim : (j + 1) * edim] = lcb[r, j] * LCB_SCALE

    for copy in copies[2:]:
        copy.wait()
    gg = og_ref[...].astype(F32) * column(gain_ref[...])
    gg_ref[...] = gg
    for k in range(own // 8):
        r, q = divmod(k, 2)
        lane = nl * edim + q * rows
        sent_ref[r * 8 : r * 8 + 8, lane : lane + rows] = gg[k * 8 : k * 8 + 8] * GG_SCALE
    out_ref[...] = sent_ref[...].astype(BF16)


def front(embeddings, projection, compress, out_grad, gain):
    samples, edim, fields = embeddings.shape
    rank, nl, block = projection.shape[1], compress.shape[1], 8
    rows, width = out_grad.shape
    total = nl * edim + (width // 2) * rows // samples + rank * fields
    steps = samples // block
    return call(
        front_kernel,
        (
            jax.ShapeDtypeStruct((samples, total), BF16),
            jax.ShapeDtypeStruct((width, rows), F32),
        ),
        embeddings,
        projection.T,
        compress.T,
        out_grad.T,
        gain.reshape(1, -1),
        flops=2 * samples * edim * fields * 144,
        nbytes=embeddings.size * 2,
        vmem=54,
        in_specs=[pl.BlockSpec(memory_space=pltpu.HBM)] * 5,
        out_specs=(pl.BlockSpec(memory_space=pltpu.VMEM),) * 2,
        scratch_shapes=[
            pltpu.VMEM((samples, edim, fields), BF16),
            pltpu.VMEM((rank, fields), BF16),
            pltpu.VMEM((nl, fields), BF16),
            pltpu.VMEM((width, rows), BF16),
            pltpu.VMEM((1, width), F32),
            pltpu.VMEM((steps, rank, block, fields), F32),
            pltpu.VMEM((steps, nl, block, edim), F32),
            pltpu.VMEM((128, fields), F32),
            pltpu.VMEM((samples, total), F32),
            pltpu.SemaphoreType.DMA((4 + steps,)),
        ],
    )


def down_kernel(place_ref, hidden_ref, w_ref, tail_ref, mine_ref, theirs_ref, lcb_ref, gg_ref, mlp):
    core, me = place_ref[0], place_ref[1]
    chips, own, rows = mine_ref.shape
    fmw = w_ref.shape[1]
    product = lax.dot_general(w_ref[...], hidden_ref[...], (((0,), (1,)), ((), ())), preferred_element_type=F32)
    mlp[...] = product.reshape(mlp.shape)
    for z in range(chips):
        mine_ref[z] = mlp[z, core]
        theirs_ref[z] = mlp[z, 1 - core].astype(BF16)
    lane = lax.broadcasted_iota(jnp.int32, (own, fmw), 1)
    line = lax.broadcasted_iota(jnp.int32, (own, fmw), 0)
    select = jnp.where(lane == line + me * own, 1.0 / LCB_SCALE, 0.0).astype(BF16)
    lcb_ref[...] = lax.dot_general(select, tail_ref[:, :fmw], NT, preferred_element_type=F32)
    for z in range(chips):
        part = tail_ref[z * own : (z + 1) * own, fmw:].astype(F32) * (1.0 / GG_SCALE)
        pieces = [part[r * 8 : r * 8 + 8, q * rows : (q + 1) * rows] for r in range(own // 8) for q in range(2)]
        gg_ref[2 * z * own : 2 * (z + 1) * own] = jnp.concatenate(pieces, axis=0).astype(BF16)


def down(place, hidden, w_down, tail, own):
    rows, fmw = hidden.shape[0], w_down.shape[1]
    chips = fmw // (2 * own)
    vmem = pl.BlockSpec(memory_space=pltpu.VMEM)
    return call(
        down_kernel,
        (
            jax.ShapeDtypeStruct((chips, own, rows), F32),
            jax.ShapeDtypeStruct((chips, own, rows), BF16),
            jax.ShapeDtypeStruct((own, rows), F32),
            jax.ShapeDtypeStruct((fmw, rows), BF16),
        ),
        place,
        hidden,
        w_down,
        tail,
        flops=2 * rows * fmw * w_down.shape[0],
        nbytes=4 * MIB,
        in_specs=[pl.BlockSpec(memory_space=pltpu.SMEM)] + [vmem] * 3,
        out_specs=(vmem,) * 4,
        scratch_shapes=[pltpu.VMEM((chips, 2, own, rows), F32)],
    )


def stats_kernel(arrived_ref, lcb_ref, gg_ref, message_ref, delta_ref):
    own, rows = arrived_ref.shape[1:]
    mlp = arrived_ref[0].astype(F32)
    for z in range(1, arrived_ref.shape[0]):
        mlp = mlp + arrived_ref[z].astype(F32)
    lcb = lcb_ref[...]
    mean = (jnp.sum(mlp, axis=0, keepdims=True) + jnp.sum(lcb, axis=0, keepdims=True)) / (2 * own)
    d0, d1 = mlp - mean, lcb - mean
    g0, g1 = gg_ref[:own], gg_ref[own:]
    dev = jnp.sum(d0 * d0, axis=0, keepdims=True) + jnp.sum(d1 * d1, axis=0, keepdims=True)
    g = jnp.sum(g0, axis=0, keepdims=True) + jnp.sum(g1, axis=0, keepdims=True)
    gd = jnp.sum(g0 * d0, axis=0, keepdims=True) + jnp.sum(g1 * d1, axis=0, keepdims=True)
    stats = jnp.concatenate([mean, dev, g, gd], axis=0)
    high = stats.astype(BF16).astype(F32)
    message_ref[...] = jnp.concatenate([d0, high, stats - high], axis=0).astype(BF16)
    delta_ref[:own], delta_ref[own : 2 * own] = d0, d1
    delta_ref[2 * own :] = jnp.broadcast_to(mean, (8, rows))


def own_stats(arrived, lcb, gg):
    _, own, rows = arrived.shape
    return call(
        stats_kernel,
        (jax.ShapeDtypeStruct((own + 8, rows), BF16), jax.ShapeDtypeStruct((2 * own + 8, rows), F32)),
        arrived,
        lcb,
        gg,
        flops=own * rows * 20,
        nbytes=arrived.size * 2,
        in_specs=[pl.BlockSpec(memory_space=pltpu.VMEM)] * 3,
        out_specs=(pl.BlockSpec(memory_space=pltpu.VMEM),) * 2,
    )


def grad_kernel(every_ref, gg_ref, hidden_ref, delta_ref, gain_ref, grad_ref, block_ref, dmix):
    tp, padded, rows = every_ref.shape
    own = padded - 8
    width = 2 * own
    full = width * tp
    deltas, numbers = [], []
    for t in range(tp):
        part = every_ref[t].astype(F32)
        deltas.append(part[:own])
        numbers.append(part[own : own + 4] + part[own + 4 :])
    mean = sum(n[0:1] for n in numbers) / tp
    shifts = [n[0:1] - mean for n in numbers]
    var = sum(n[1:2] + width * s * s for n, s in zip(numbers, shifts)) / full
    rstd = 1.0 / jnp.sqrt(var + 1e-05)
    first = sum(n[2:3] for n in numbers) / full
    second = sum(n[3:4] + s * n[2:3] for n, s in zip(numbers, shifts)) * rstd / full
    scale = rstd * second
    for t in range(tp):
        offset = first + shifts[t] * scale
        g = gg_ref[t * own : (t + 1) * own].astype(F32)
        dmix[t * own : (t + 1) * own] = ((g - offset - deltas[t] * scale) * rstd).astype(BF16)
    grad_ref[...] = lax.dot_general(
        hidden_ref[...], dmix[...], (((0,), (1,)), ((), ())), preferred_element_type=F32
    ).astype(BF16)
    shift = delta_ref[width : width + 1] - mean
    block_ref[...] = ((delta_ref[:width] + shift) * rstd * column(gain_ref[...])).astype(BF16)


def down_gradient(every, gg, hidden, delta, gain):
    tp, padded, rows = every.shape
    fmw, width = gg.shape[0], 2 * (padded - 8)
    return call(
        grad_kernel,
        (jax.ShapeDtypeStruct((hidden.shape[1], fmw), BF16), jax.ShapeDtypeStruct((width, rows), BF16)),
        every,
        gg,
        hidden,
        delta,
        gain.reshape(1, -1),
        flops=2 * rows * fmw * hidden.shape[1],
        nbytes=3 * MIB,
        in_specs=[pl.BlockSpec(memory_space=pltpu.VMEM)] * 5,
        out_specs=(pl.BlockSpec(memory_space=pltpu.VMEM),) * 2,
        scratch_shapes=[pltpu.VMEM((fmw, rows), BF16)],
    )


def on_device(embeddings, projection, compress, w_up, w_down, output_norm_gain, out_grad):
    tp = lax.axis_size("tp")
    dp = lax.axis_size("dp")
    me = lax.axis_index("tp")
    feat, fmw = w_up.shape[0], w_down.shape[1]
    own = fmw // tp

    sent, gg = front(embeddings, projection, compress, out_grad, output_norm_gain)
    got = lax.all_gather(sent.astype(F16), "tp", axis=0, tiled=True)

    pre = jnp.dot(got[:, 2 * fmw :].astype(BF16), w_up, preferred_element_type=F32)
    hidden = jax.nn.gelu(pre * (1.0 / NORMED_SCALE), approximate=True).astype(BF16)
    tail = got[:, : 2 * fmw].astype(BF16)

    place = jnp.stack([me % 2, me]).astype(jnp.int32)
    mine, theirs, lcb_own, gg_all = down(place, hidden, w_down, tail, own)
    swap = [(i, i ^ 1) for i in range(tp)]
    chip_sum = (mine + lax.ppermute(theirs, "tp", swap).astype(F32)).astype(BF16)
    same_core = [list(range(c, tp, 2)) for c in range(2)]
    arrived = lax.all_to_all(chip_sum, "tp", 0, 0, tiled=True, axis_index_groups=same_core)

    message, delta = own_stats(arrived, lcb_own, gg)
    every = lax.all_gather(message, "tp", axis=0, tiled=False)
    grad, block = down_gradient(every, gg_all, hidden, delta, output_norm_gain)
    parts = lax.all_to_all(grad.reshape(dp, -1, fmw), "dp", 0, 0, tiled=True)
    return block.T, parts.astype(F32).sum(axis=0)


def solution(mesh):
    return jax.shard_map(
        on_device,
        mesh=mesh,
        in_specs=(
            P(("dp", "tp"), None, None),
            P(),
            P(),
            P(None, "tp"),
            P("tp", None),
            P("tp"),
            P("dp", "tp"),
        ),
        out_specs=(P("dp", "tp"), P(("tp", "dp"), None)),
        check_vma=False,
    )
```

time: 121 us -> 112 us (0.926)
  blocking collectives: 55.3 us -> 96.3 us
  waiting for transfers between devices: 23.5 us -> 1.19 us
  starting transfers between devices: 16.5 us -> 2.28 us
  local copies, waits for them, and re-layouts: 10.6 us -> 1.01 us
  Pallas kernels: 0 us -> 7.53 us
  other arithmetic: 8.4 us -> 1.94 us
  matrix products: 5.05 us -> 1.08 us
    all_to_all x0 -> x2, blocking collectives: none -> 41.1 us  [the longest x1 25.4 us: on_device(): parts = lax.all_to_all(grad.reshape(dp, -1, fmw), 'dp', 0, 0, tiled=True)]
    all_to_all x2 -> x0, waiting for transfers between devices: 22.4 us -> none  [the longest x1 14.7 us: on_device(): parts = lax.all_to_all(grad.reshape(dp, -1, fmw), 'dp', 0, 0, tiled=True)]
    all_to_all x2 -> x0, starting transfers between devices: 14.2 us -> none  [the longest x1 10.2 us: on_device(): parts = lax.all_to_all(grad.reshape(dp, -1, fmw), 'dp', 0, 0, tiled=True)]
    pallas_call x0 -> x4, Pallas kernels: none -> 7.53 us  [call(): pl.pallas_call(kernel, out_shape=out_shape, compiler_params=pltpu.Compile...]
    dot_general x5 -> x1, matrix products: 5.05 us -> 1.08 us  [on_device(): jnp.dot(got[:, 2 * fmw:].astype(BF16), w_up, preferred_element_type=F32)]
    unnamed x26 -> x8, local copies, waits for them, and re-layouts: 4.87 us -> 1.01 us
    mul x2 -> x0, local copies, waits for them, and re-layouts: 2.98 us -> none  [on_device(): gg_all.astype(F32) * (1.0 / GG_SCALE) - first - xhat * second]
    reduce_sum x7 -> x1, other arithmetic: 3.4 us -> 0.67 us  [on_device(): return (block.T, parts.astype(F32).sum(axis=0))]
  transfers between devices with their start and end apart: 3 -> 1, of which waited for: 3 -> 1; matrix products, arithmetic and copies ran while one was open for 5% -> 0% of each run, Pallas kernels for 0% -> 0%
where the time goes in v2:
time: 112 us
  blocking collectives  96.3 us (86%)
  Pallas kernels  7.53 us (7%)
  starting transfers between devices  2.28 us (2%)
  other arithmetic  1.94 us (2%)
  waiting for transfers between devices  1.19 us (1%)
    all_gather x1, blocking collectives, on_device(): got = lax.all_gather(sent.astype(F16), 'tp', axis=0, tiled=True)  38.6 us
    all_to_all x1, blocking collectives, on_device(): parts = lax.all_to_all(grad.reshape(dp, -1, fmw), 'dp', 0, 0, tiled=True)  25.4 us
    all_gather x1, blocking collectives, on_device(): every = lax.all_gather(message, 'tp', axis=0, tiled=False)  16.6 us
    all_to_all x1, blocking collectives, on_device(): lax.all_to_all(chip_sum, 'tp', 0, 0, tiled=True, axis_index_groups=same_c...  15.8 us
    pallas_call x4, Pallas kernels, call(): pl.pallas_call(kernel, out_shape=out_shape, compiler_params=pltpu.Compile...  7.53 us
    ppermute x1, starting transfers between devices, on_device(): lax.ppermute(theirs, 'tp', swap).astype(F32)  2.28 us
  transfers between devices with their start and end apart: 1, of which 1 were waited for; matrix products, arithmetic and copies ran while one was open for 0% of the time, Pallas kernels for 0%

profile of v2, /device:TPU:8, one launch (start us, length us, event | category | flops | bytes accessed | tf_op | source)
XLA Modules:
  0.0 112.0 jit_solution(10726055056547786615)
XLA Ops:
  0.6 0.0 copy-start
  0.7 5.1 %shard_map.86 = (bf16[24,5632]{1,0:T(8,128)(2,1)}, f32[96,384]{1,0:T(8,128)}) custom-call(bf16[24,192,256]{2,1,0:T(8,128)(2,1)} %refs_0_.1, bf16[16,256]{1,0:T(8,128)(2,1)} %bitcast.15, bf16[4,256]{1,0:T(4,128)(2,1)} %bitcast.16, bf16[96,384]{1,0:T(8,128)(2,1)} %bitcast.14, f32[1,96]{1,0:T(1,128)} %bitcast.12), custom_call_target="tpu_custom_call" | custom-call | flops 339738624 | bytes 2359296 | tf_op jit(solution)/shard_map/pallas_call | solution.py:15
  5.8 1.0 convert_element_type.21
  6.8 38.6 %all-gather.2 = f16[384,5632]{1,0:T(8,128)(2,1)S(1)} all-gather(f16[24,5632]{1,0:T(8,128)(2,1)S(1)} %convert_element_type.21), channel_id=1, replica_groups=mesh['dp'=32,'tp'=16] {'tp'}, dimensions={0}, use_global_device_ids=true | all-gather | bytes 4595712 | tf_op jit(solution)/shard_map/all_gather | solution.py:257
  45.3 0.1 slice_convert_fusion.4.tail_ref
  45.5 0.0 copy-done
  45.5 1.1 fusion.9.hidden_ref
  46.6 0.1 pad_add_fusion.place_ref
  46.7 0.0 copy-start.1
  46.7 1.0 copy-done.1
  47.7 0.0 copy-start.2
  47.7 0.0 copy-start.3
  47.7 1.1 shard_map.87
  48.8 2.3 %collective-permute-start = (bf16[8,48,384]{2,1,0:T(8,128)(2,1)S(1)}, bf16[8,48,384]{2,1,0:T(8,128)(2,1)S(1)}, u32[]{:S(2)}, u32[]{:S(2)}) collective-permute-start(bf16[8,48,384]{2,1,0:T(8,128)(2,1)S(1)} %get-tuple-element.14), channel_id=1, source_target_pairs={{0,1},{1,0},{2,3},{3,2},{4,5},{5,4},{6,7},{7,6},{8,9},{9,8},{10,11... | collective-permute-start | bytes 884744 | tf_op jit(solution)/shard_map/ppermute | solution.py:266
  51.1 1.2 %collective-permute-done = bf16[8,48,384]{2,1,0:T(8,128)(2,1)S(1)} collective-permute-done((bf16[8,48,384]{2,1,0:T(8,128)(2,1)S(1)}, bf16[8,48,384]{2,1,0:T(8,128)(2,1)S(1)}, u32[]{:S(2)}, u32[]{:S(2)}) %collective-permute-start) | collective-permute-done | bytes 294944 | tf_op jit(solution)/shard_map/ppermute | solution.py:266
  52.3 0.1 add_convert_fusion
  52.3 15.8 %all_to_all.10.arrived_ref = bf16[8,48,384]{2,1,0:T(8,128)(2,1)S(1)} all-to-all(bf16[8,48,384]{2,1,0:T(8,128)(2,1)S(1)} %add_convert_fusion), channel_id=1, replica_groups={{0,2,4,6,8,10,12,14},{1,3,5,7,9,11,13,15},{16,18,20,22,24,26,28,30},{17..., dimensions={0} | all-to-all | bytes 589824 | tf_op jit(solution)/shard_map/all_to_all | solution.py:268
  68.1 0.0 copy-done.2
  68.1 0.1 shard_map.88
  68.2 16.6 %all-gather = bf16[896,384]{1,0:T(8,128)(2,1)S(1)} all-gather(bf16[56,384]{1,0:T(8,128)(2,1)S(1)} %get-tuple-element.17), channel_id=2, replica_groups=mesh['dp'=32,'tp'=16] {'tp'}, dimensions={0}, use_global_device_ids=true | all-gather | bytes 731136 | tf_op jit(solution)/shard_map/all_gather | solution.py:271
  84.8 0.0 copy-done.3
  84.8 1.2 %shard_map.89 = (bf16[256,768]{1,0:T(8,128)(2,1)S(1)}, bf16[96,384]{1,0:T(8,128)(2,1)}) custom-call(bf16[16,56,384]{2,1,0:T(8,128)(2,1)S(1)} %bitcast.10, bf16[768,384]{1,0:T(8,128)(2,1)S(1)} %get-tuple-element.18.gg_ref, bf16[384,256]{1,0:T(8,128)(2,1)S(1)} %fusion.9.hidden_ref, f32[104,384]{1,0:T(8,128)S(1)} %get-tuple-element.19.delta_ref, ...), custom_call_target="tpu_custom_call" | custom-call | flops 150994944 | bytes 3145728 | tf_op jit(solution)/shard_map/pallas_call | solution.py:15
  86.0 25.4 %all_to_all.11 = bf16[32,8,768]{2,1,0:T(8,128)(2,1)S(1)} all-to-all(bf16[32,8,768]{2,1,0:T(8,128)(2,1)S(1)} %bitcast.11), channel_id=1, replica_groups=mesh['dp'=32,'tp'=16] {'dp'}, dimensions={0} | all-to-all | bytes 786432 | tf_op jit(solution)/shard_map/all_to_all | solution.py:273
  111.4 0.7 convert_reduce_fusion
Async XLA Ops:
  0.6 44.8 %copy-start = (bf16[4096,256]{1,0:T(8,128)(2,1)S(1)}, bf16[4096,256]{1,0:T(8,128)(2,1)}, u32[]{:S(2)}) copy-start(bf16[4096,256]{1,0:T(8,128)(2,1)} %param.10) | copy-start | bytes 6291460
  46.7 1.0 copy-start.1
  47.7 20.4 %copy-start.2 = (f32[96,384]{1,0:T(8,128)S(1)}, f32[96,384]{1,0:T(8,128)}, u32[]{:S(2)}) copy-start(f32[96,384]{1,0:T(8,128)} %get-tuple-element.16.gg_ref) | copy-start | bytes 442372
  47.7 37.1 %copy-start.3 = (f32[96]{0:T(128)S(1)}, f32[96]{0:T(128)}, u32[]{:S(2)}) copy-start(f32[96]{0:T(128)} %param.12) | copy-start | bytes 1156
  48.8 3.5 %collective-permute-start = (bf16[8,48,384]{2,1,0:T(8,128)(2,1)S(1)}, bf16[8,48,384]{2,1,0:T(8,128)(2,1)S(1)}, u32[]{:S(2)}, u32[]{:S(2)}) collective-permute-start(bf16[8,48,384]{2,1,0:T(8,128)(2,1)S(1)} %get-tuple-element.14), channel_id=1, source_target_pairs={{0,1},{1,0},{2,3},{3,2},{4,5},{5,4},{6,7},{7,6},{8,9},{9,8},{10,11... | collective-permute-start | bytes 884744 | tf_op jit(solution)/shard_map/ppermute | solution.py:266

commit v3 on v2

--- a/solution.py
+++ b/solution.py
@@ -6,7 +6,7 @@
 from jax.sharding import PartitionSpec as P
 
 BF16, F16, F32 = jnp.bfloat16, jnp.float16, jnp.float32
-NORMED_SCALE, LCB_SCALE, GG_SCALE = 512.0, 64.0, 4096.0
+NORMED_SCALE, GG_SCALE = 512.0, 4096.0
 NT = (((1,), (1,)), ((), ()))
 MIB = 1 << 20
 
@@ -27,7 +27,7 @@
 
 def front_kernel(*refs):
     sources, refs = refs[:5], refs[5:]
-    out_ref, gg_ref, x_ref, projection_ref, compress_ref, og_ref, gain_ref, inter, lcb, w, sent_ref, sems = refs
+    out_ref, lcb_ref, gg_ref, x_ref, projection_ref, compress_ref, og_ref, gain_ref, inter, lcb, w, sent_ref, sems = refs
     samples, edim, fields = x_ref.shape
     steps, rank, block = inter.shape[:3]
     nl = lcb.shape[1]
@@ -53,7 +53,7 @@
     copies[1].wait()
     w[:rank] = projection_ref[...].astype(F32)
     w[rank : rank + nl] = compress_ref[...].astype(F32)
-    start = nl * edim + own * rows // samples
+    start = own * rows // samples
     for r in range(steps):
         chunks[r].wait()
         x = x_ref[r * block : (r + 1) * block]
@@ -72,7 +72,7 @@
         for k in range(rank):
             sent_ref[at, start + k * fields : start + (k + 1) * fields] = lines[k] * factor
         for j in range(nl):
-            sent_ref[at, j * edim : (j + 1) * edim] = lcb[r, j] * LCB_SCALE
+            lcb_ref[at, j * edim : (j + 1) * edim] = lcb[r, j]
 
     for copy in copies[2:]:
         copy.wait()
@@ -80,8 +80,7 @@
     gg_ref[...] = gg
     for k in range(own // 8):
         r, q = divmod(k, 2)
-        lane = nl * edim + q * rows
-        sent_ref[r * 8 : r * 8 + 8, lane : lane + rows] = gg[k * 8 : k * 8 + 8] * GG_SCALE
+        sent_ref[r * 8 : r * 8 + 8, q * rows : (q + 1) * rows] = gg[k * 8 : k * 8 + 8] * GG_SCALE
     out_ref[...] = sent_ref[...].astype(BF16)
 
 
@@ -89,12 +88,13 @@
     samples, edim, fields = embeddings.shape
     rank, nl, block = projection.shape[1], compress.shape[1], 8
     rows, width = out_grad.shape
-    total = nl * edim + (width // 2) * rows // samples + rank * fields
+    total = (width // 2) * rows // samples + rank * fields
     steps = samples // block
     return call(
         front_kernel,
         (
             jax.ShapeDtypeStruct((samples, total), BF16),
+            jax.ShapeDtypeStruct((samples, nl * edim), F32),
             jax.ShapeDtypeStruct((width, rows), F32),
         ),
         embeddings,
@@ -106,7 +106,7 @@
         nbytes=embeddings.size * 2,
         vmem=54,
         in_specs=[pl.BlockSpec(memory_space=pltpu.HBM)] * 5,
-        out_specs=(pl.BlockSpec(memory_space=pltpu.VMEM),) * 2,
+        out_specs=(pl.BlockSpec(memory_space=pltpu.VMEM),) * 3,
         scratch_shapes=[
             pltpu.VMEM((samples, edim, fields), BF16),
             pltpu.VMEM((rank, fields), BF16),
@@ -122,55 +122,71 @@
     )
 
 
-def down_kernel(place_ref, hidden_ref, w_ref, tail_ref, mine_ref, theirs_ref, lcb_ref, gg_ref, mlp):
-    core, me = place_ref[0], place_ref[1]
-    chips, own, rows = mine_ref.shape
-    fmw = w_ref.shape[1]
+def down_kernel(place_ref, hidden_ref, w_ref, tail_ref, local_ref, mine_ref, theirs_ref, gg_ref, mlp):
+    core, chip = place_ref[0], place_ref[1]
+    chips, padded, rows = mine_ref.shape
+    own = padded - 8
+    samples, fmw = local_ref.shape
     product = lax.dot_general(w_ref[...], hidden_ref[...], (((0,), (1,)), ((), ())), preferred_element_type=F32)
-    mlp[...] = product.reshape(mlp.shape)
+    mlp[:, :, :own] = product.reshape(chips, 2, own, rows)
+    turned = local_ref[...].T
+    lane = lax.broadcasted_iota(jnp.int32, (samples, rows), 1)
+    line = lax.broadcasted_iota(jnp.int32, (samples, rows), 0)
+    packed = jnp.zeros((2 * chips * 8, rows), F32)
+    for k in range(own // 8):
+        lines = [turned[g * own + k * 8 : g * own + k * 8 + 8] for g in range(2 * chips)]
+        first = ((k + chip) % chips * 2 + core) * samples
+        spot = jnp.where(lane == line + first, 1.0, 0.0).astype(BF16)
+        packed += jnp.dot(jnp.concatenate(lines, axis=0).astype(BF16), spot, preferred_element_type=F32)
+    mlp[:, :, own:] = packed.reshape(chips, 2, 8, rows)
     for z in range(chips):
         mine_ref[z] = mlp[z, core]
         theirs_ref[z] = mlp[z, 1 - core].astype(BF16)
-    lane = lax.broadcasted_iota(jnp.int32, (own, fmw), 1)
-    line = lax.broadcasted_iota(jnp.int32, (own, fmw), 0)
-    select = jnp.where(lane == line + me * own, 1.0 / LCB_SCALE, 0.0).astype(BF16)
-    lcb_ref[...] = lax.dot_general(select, tail_ref[:, :fmw], NT, preferred_element_type=F32)
     for z in range(chips):
-        part = tail_ref[z * own : (z + 1) * own, fmw:].astype(F32) * (1.0 / GG_SCALE)
+        part = tail_ref[z * own : (z + 1) * own].astype(F32) * (1.0 / GG_SCALE)
         pieces = [part[r * 8 : r * 8 + 8, q * rows : (q + 1) * rows] for r in range(own // 8) for q in range(2)]
         gg_ref[2 * z * own : 2 * (z + 1) * own] = jnp.concatenate(pieces, axis=0).astype(BF16)
 
 
-def down(place, hidden, w_down, tail, own):
+def down(place, hidden, w_down, tail, local, own):
     rows, fmw = hidden.shape[0], w_down.shape[1]
     chips = fmw // (2 * own)
     vmem = pl.BlockSpec(memory_space=pltpu.VMEM)
     return call(
         down_kernel,
         (
-            jax.ShapeDtypeStruct((chips, own, rows), F32),
-            jax.ShapeDtypeStruct((chips, own, rows), BF16),
-            jax.ShapeDtypeStruct((own, rows), F32),
+            jax.ShapeDtypeStruct((chips, own + 8, rows), F32),
+            jax.ShapeDtypeStruct((chips, own + 8, rows), BF16),
             jax.ShapeDtypeStruct((fmw, rows), BF16),
         ),
         place,
         hidden,
         w_down,
         tail,
+        local,
         flops=2 * rows * fmw * w_down.shape[0],
         nbytes=4 * MIB,
-        in_specs=[pl.BlockSpec(memory_space=pltpu.SMEM)] + [vmem] * 3,
-        out_specs=(vmem,) * 4,
-        scratch_shapes=[pltpu.VMEM((chips, 2, own, rows), F32)],
-    )
-
-
-def stats_kernel(arrived_ref, lcb_ref, gg_ref, message_ref, delta_ref):
-    own, rows = arrived_ref.shape[1:]
-    mlp = arrived_ref[0].astype(F32)
-    for z in range(1, arrived_ref.shape[0]):
-        mlp = mlp + arrived_ref[z].astype(F32)
-    lcb = lcb_ref[...]
+        in_specs=[pl.BlockSpec(memory_space=pltpu.SMEM)] + [vmem] * 4,
+        out_specs=(vmem,) * 3,
+        scratch_shapes=[pltpu.VMEM((chips, 2, own + 8, rows), F32)],
+    )
+
+
+def stats_kernel(arrived_ref, gg_ref, message_ref, delta_ref):
+    chips, padded, rows = arrived_ref.shape
+    own = padded - 8
+    arrived = [arrived_ref[z].astype(F32) for z in range(chips)]
+    mlp = sum(a[:own] for a in arrived)
+    lane = lax.broadcasted_iota(jnp.int32, (8, rows), 1)
+    span = rows // chips
+    blocks = [(lane >= span * b) & (lane < span * (b + 1)) for b in range(chips)]
+    lines = []
+    for k in range(own // 8):
+        line = jnp.zeros((8, rows), F32)
+        for z in range(chips):
+            line = jnp.where(blocks[(k + z) % chips], arrived[z][own:], line)
+        lines.append(pltpu.roll(line, (rows - span * k) % rows, 1) if k else line)
+    lcb = jnp.concatenate(lines, axis=0)
     mean = (jnp.sum(mlp, axis=0, keepdims=True) + jnp.sum(lcb, axis=0, keepdims=True)) / (2 * own)
     d0, d1 = mlp - mean, lcb - mean
     g0, g1 = gg_ref[:own], gg_ref[own:]
@@ -184,17 +200,17 @@
     delta_ref[2 * own :] = jnp.broadcast_to(mean, (8, rows))
 
 
-def own_stats(arrived, lcb, gg):
-    _, own, rows = arrived.shape
+def own_stats(arrived, gg):
+    _, padded, rows = arrived.shape
+    own = padded - 8
     return call(
         stats_kernel,
         (jax.ShapeDtypeStruct((own + 8, rows), BF16), jax.ShapeDtypeStruct((2 * own + 8, rows), F32)),
         arrived,
-        lcb,
         gg,
         flops=own * rows * 20,
         nbytes=arrived.size * 2,
-        in_specs=[pl.BlockSpec(memory_space=pltpu.VMEM)] * 3,
+        in_specs=[pl.BlockSpec(memory_space=pltpu.VMEM)] * 2,
         out_specs=(pl.BlockSpec(memory_space=pltpu.VMEM),) * 2,
     )
 
@@ -253,21 +269,21 @@
     feat, fmw = w_up.shape[0], w_down.shape[1]
     own = fmw // tp
 
-    sent, gg = front(embeddings, projection, compress, out_grad, output_norm_gain)
+    sent, local, gg = front(embeddings, projection, compress, out_grad, output_norm_gain)
     got = lax.all_gather(sent.astype(F16), "tp", axis=0, tiled=True)
 
-    pre = jnp.dot(got[:, 2 * fmw :].astype(BF16), w_up, preferred_element_type=F32)
+    pre = jnp.dot(got[:, fmw:].astype(BF16), w_up, preferred_element_type=F32)
     hidden = jax.nn.gelu(pre * (1.0 / NORMED_SCALE), approximate=True).astype(BF16)
-    tail = got[:, : 2 * fmw].astype(BF16)
-
-    place = jnp.stack([me % 2, me]).astype(jnp.int32)
-    mine, theirs, lcb_own, gg_all = down(place, hidden, w_down, tail, own)
+    tail = got[:, :fmw].astype(BF16)
+
+    place = jnp.stack([me % 2, me // 2]).astype(jnp.int32)
+    mine, theirs, gg_all = down(place, hidden, w_down, tail, local, own)
     swap = [(i, i ^ 1) for i in range(tp)]
     chip_sum = (mine + lax.ppermute(theirs, "tp", swap).astype(F32)).astype(BF16)
     same_core = [list(range(c, tp, 2)) for c in range(2)]
     arrived = lax.all_to_all(chip_sum, "tp", 0, 0, tiled=True, axis_index_groups=same_core)
 
-    message, delta = own_stats(arrived, lcb_own, gg)
+    message, delta = own_stats(arrived, gg)
     every = lax.all_gather(message, "tp", axis=0, tiled=False)
     grad, block = down_gradient(every, gg_all, hidden, delta, output_norm_gain)
     parts = lax.all_to_all(grad.reshape(dp, -1, fmw), "dp", 0, 0, tiled=True)

time: 112 us -> 110 us (0.982)
  blocking collectives: 96.3 us -> 94.5 us
    all_gather x1, blocking collectives: 38.6 us -> 35.7 us  [on_device(): got = lax.all_gather(sent.astype(F16), 'tp', axis=0, tiled=True)]
where the time goes in v3:
time: 110 us; the launch traced here: 109 us
  blocking collectives  94.5 us (86%)
  Pallas kernels  7.67 us (7%)
  starting transfers between devices  2.28 us (2%)
  other arithmetic  1.88 us (2%)
  waiting for transfers between devices  1.26 us (1%)
    all_gather x1, blocking collectives, on_device(): got = lax.all_gather(sent.astype(F16), 'tp', axis=0, tiled=True)  35.7 us
    all_to_all x1, blocking collectives, on_device(): parts = lax.all_to_all(grad.reshape(dp, -1, fmw), 'dp', 0, 0, tiled=True)  25.4 us
    all_to_all x1, blocking collectives, on_device(): lax.all_to_all(chip_sum, 'tp', 0, 0, tiled=True, axis_index_groups=same_c...  16.8 us
    all_gather x1, blocking collectives, on_device(): every = lax.all_gather(message, 'tp', axis=0, tiled=False)  16.6 us
    pallas_call x4, Pallas kernels, call(): pl.pallas_call(kernel, out_shape=out_shape, compiler_params=pltpu.Compile...  7.67 us
    ppermute x1, starting transfers between devices, on_device(): lax.ppermute(theirs, 'tp', swap).astype(F32)  2.28 us
  transfers between devices with their start and end apart: 1, of which 1 were waited for; matrix products, arithmetic and copies ran while one was open for 0% of the time, Pallas kernels for 0%

profile of v3, /device:TPU:8, one launch (start us, length us, event | category | flops | bytes accessed | tf_op | source)
XLA Modules:
  0.0 109.5 jit_solution(8660508020839902078)
XLA Ops:
  0.6 0.0 copy-start
  0.7 5.1 %shard_map.86 = (bf16[24,4864]{1,0:T(8,128)(2,1)}, f32[24,768]{1,0:T(8,128)}, f32[96,384]{1,0:T(8,128)}) custom-call(bf16[24,192,256]{2,1,0:T(8,128)(2,1)} %refs_0_.1, bf16[16,256]{1,0:T(8,128)(2,1)} %bitcast.15, bf16[4,256]{1,0:T(4,128)(2,1)} %bitcast.16, bf16[96,384]{1,0:T(8,128)(2,1)} %bitcast.14, f32[1,96]{1,0:T(1,128)} %bitcast.12), custom_call_target="tpu_custom_call" | custom-call | flops 339738624 | bytes 2359296 | tf_op jit(solution)/shard_map/pallas_call | solution.py:15
  5.7 1.0 convert_element_type.21
  6.7 35.7 %all-gather.2 = f16[384,4864]{1,0:T(8,128)(2,1)S(1)} all-gather(f16[24,4864]{1,0:T(8,128)(2,1)S(1)} %convert_element_type.21), channel_id=1, replica_groups=mesh['dp'=32,'tp'=16] {'tp'}, dimensions={0}, use_global_device_ids=true | all-gather | bytes 3969024 | tf_op jit(solution)/shard_map/all_gather | solution.py:273
  42.5 0.1 slice_convert_fusion.4.tail_ref
  42.5 0.0 copy-done
  42.5 0.0 copy-start.1
  42.5 0.0 copy-start.3
  42.6 1.1 fusion.9.hidden_ref
  43.6 0.0 copy-start.2
  43.6 0.0 copy-start.4
  43.7 0.1 pad_add_fusion.place_ref
  43.7 0.0 copy-done.1
  43.7 0.0 copy-done.3
  43.7 1.3 %shard_map.87 = (f32[8,56,384]{2,1,0:T(8,128)S(1)}, bf16[8,56,384]{2,1,0:T(8,128)(2,1)S(1)}, bf16[768,384]{1,0:T(8,128)(2,1)S(1)}) custom-call(s32[2]{0:T(128)S(1)} %pad_add_fusion.place_ref, bf16[384,256]{1,0:T(8,128)(2,1)S(1)} %fusion.9.hidden_ref, bf16[256,768]{1,0:T(8,128)(2,1)S(1)} %copy-done.1, bf16[384,768]{1,0:T(8,128)(2,1)S(1)} %slice_convert_fusion.4.tail_ref, ...), custom_call_target="tpu_custom_call" | custom-call | flops 150994944 | bytes 4194304 | tf_op jit(solution)/shard_map/pallas_call | solution.py:15
  45.0 2.3 %collective-permute-start = (bf16[8,56,384]{2,1,0:T(8,128)(2,1)S(1)}, bf16[8,56,384]{2,1,0:T(8,128)(2,1)S(1)}, u32[]{:S(2)}, u32[]{:S(2)}) collective-permute-start(bf16[8,56,384]{2,1,0:T(8,128)(2,1)S(1)} %get-tuple-element.15), channel_id=1, source_target_pairs={{0,1},{1,0},{2,3},{3,2},{4,5},{5,4},{6,7},{7,6},{8,9},{9,8},{10,11... | collective-permute-start | bytes 1032200 | tf_op jit(solution)/shard_map/ppermute | solution.py:282
  47.3 1.3 %collective-permute-done = bf16[8,56,384]{2,1,0:T(8,128)(2,1)S(1)} collective-permute-done((bf16[8,56,384]{2,1,0:T(8,128)(2,1)S(1)}, bf16[8,56,384]{2,1,0:T(8,128)(2,1)S(1)}, u32[]{:S(2)}, u32[]{:S(2)}) %collective-permute-start) | collective-permute-done | bytes 344096 | tf_op jit(solution)/shard_map/ppermute | solution.py:282
  48.6 0.1 add_convert_fusion
  48.6 16.8 %all_to_all.10.arrived_ref = bf16[8,56,384]{2,1,0:T(8,128)(2,1)S(1)} all-to-all(bf16[8,56,384]{2,1,0:T(8,128)(2,1)S(1)} %add_convert_fusion), channel_id=1, replica_groups={{0,2,4,6,8,10,12,14},{1,3,5,7,9,11,13,15},{16,18,20,22,24,26,28,30},{17..., dimensions={0} | all-to-all | bytes 688128 | tf_op jit(solution)/shard_map/all_to_all | solution.py:284
  65.5 0.0 copy-done.2
  65.5 0.1 shard_map.88
  65.6 16.6 %all-gather = bf16[896,384]{1,0:T(8,128)(2,1)S(1)} all-gather(bf16[56,384]{1,0:T(8,128)(2,1)S(1)} %get-tuple-element.17), channel_id=2, replica_groups=mesh['dp'=32,'tp'=16] {'tp'}, dimensions={0}, use_global_device_ids=true | all-gather | bytes 731136 | tf_op jit(solution)/shard_map/all_gather | solution.py:287
  82.2 0.0 copy-done.4
  82.2 1.2 %shard_map.89 = (bf16[256,768]{1,0:T(8,128)(2,1)S(1)}, bf16[96,384]{1,0:T(8,128)(2,1)}) custom-call(bf16[16,56,384]{2,1,0:T(8,128)(2,1)S(1)} %bitcast.10, bf16[768,384]{1,0:T(8,128)(2,1)S(1)} %get-tuple-element.18.gg_ref, bf16[384,256]{1,0:T(8,128)(2,1)S(1)} %fusion.9.hidden_ref, f32[104,384]{1,0:T(8,128)S(1)} %get-tuple-element.19.delta_ref, ...), custom_call_target="tpu_custom_call" | custom-call | flops 150994944 | bytes 3145728 | tf_op jit(solution)/shard_map/pallas_call | solution.py:15
  83.4 25.4 %all_to_all.11 = bf16[32,8,768]{2,1,0:T(8,128)(2,1)S(1)} all-to-all(bf16[32,8,768]{2,1,0:T(8,128)(2,1)S(1)} %bitcast.11), channel_id=1, replica_groups=mesh['dp'=32,'tp'=16] {'dp'}, dimensions={0} | all-to-all | bytes 786432 | tf_op jit(solution)/shard_map/all_to_all | solution.py:289
  108.8 0.7 convert_reduce_fusion
Async XLA Ops:
  0.6 41.9 %copy-start = (bf16[4096,256]{1,0:T(8,128)(2,1)S(1)}, bf16[4096,256]{1,0:T(8,128)(2,1)}, u32[]{:S(2)}) copy-start(bf16[4096,256]{1,0:T(8,128)(2,1)} %param.10) | copy-start | bytes 6291460
  42.5 1.2 %copy-start.1 = (bf16[256,768]{1,0:T(8,128)(2,1)S(1)}, bf16[256,768]{1,0:T(8,128)(2,1)}, u32[]{:S(2)}) copy-start(bf16[256,768]{1,0:T(8,128)(2,1)} %w_ref.1) | copy-start | bytes 1179652
  42.5 1.2 %copy-start.3 = (f32[24,768]{1,0:T(8,128)S(1)}, f32[24,768]{1,0:T(8,128)}, u32[]{:S(2)}) copy-start(f32[24,768]{1,0:T(8,128)} %get-tuple-element.13.local_ref) | copy-start | bytes 221188
  43.6 21.8 %copy-start.2 = (f32[96,384]{1,0:T(8,128)S(1)}, f32[96,384]{1,0:T(8,128)}, u32[]{:S(2)}) copy-start(f32[96,384]{1,0:T(8,128)} %get-tuple-element.16.gg_ref) | copy-start | bytes 442372
  43.6 38.6 %copy-start.4 = (f32[96]{0:T(128)S(1)}, f32[96]{0:T(128)}, u32[]{:S(2)}) copy-start(f32[96]{0:T(128)} %param.12) | copy-start | bytes 1156
  45.0 3.5 %collective-permute-start = (bf16[8,56,384]{2,1,0:T(8,128)(2,1)S(1)}, bf16[8,56,384]{2,1,0:T(8,128)(2,1)S(1)}, u32[]{:S(2)}, u32[]{:S(2)}) collective-permute-start(bf16[8,56,384]{2,1,0:T(8,128)(2,1)S(1)} %get-tuple-element.15), channel_id=1, source_target_pairs={{0,1},{1,0},{2,3},{3,2},{4,5},{5,4},{6,7},{7,6},{8,9},{9,8},{10,11... | collective-permute-start | bytes 1032200 | tf_op jit(solution)/shard_map/ppermute | solution.py:282

commit v4 on v3

--- a/solution.py
+++ b/solution.py
@@ -97,14 +97,10 @@
             jax.ShapeDtypeStruct((samples, nl * edim), F32),
             jax.ShapeDtypeStruct((width, rows), F32),
         ),
-        embeddings,
-        projection.T,
-        compress.T,
-        out_grad.T,
-        gain.reshape(1, -1),
+        *(pltpu.with_memory_space_constraint(x, pltpu.HBM) for x in (embeddings, projection.T, compress.T, out_grad.T, gain.reshape(1, -1))),
         flops=2 * samples * edim * fields * 144,
         nbytes=embeddings.size * 2,
-        vmem=54,
+        vmem=16,
         in_specs=[pl.BlockSpec(memory_space=pltpu.HBM)] * 5,
         out_specs=(pl.BlockSpec(memory_space=pltpu.VMEM),) * 3,
         scratch_shapes=[
@@ -122,8 +118,9 @@
     )
 
 
-def down_kernel(place_ref, hidden_ref, w_ref, tail_ref, local_ref, mine_ref, theirs_ref, gg_ref, mlp):
-    core, chip = place_ref[0], place_ref[1]
+def down_kernel(hidden_ref, w_ref, tail_ref, local_ref, mine_ref, theirs_ref, gg_ref, mlp):
+    me = lax.axis_index("tp")
+    core, chip = me % 2, me // 2
     chips, padded, rows = mine_ref.shape
     own = padded - 8
     samples, fmw = local_ref.shape
@@ -148,7 +145,7 @@
         gg_ref[2 * z * own : 2 * (z + 1) * own] = jnp.concatenate(pieces, axis=0).astype(BF16)
 
 
-def down(place, hidden, w_down, tail, local, own):
+def down(hidden, w_down, tail, local, own):
     rows, fmw = hidden.shape[0], w_down.shape[1]
     chips = fmw // (2 * own)
     vmem = pl.BlockSpec(memory_space=pltpu.VMEM)
@@ -159,16 +156,34 @@
             jax.ShapeDtypeStruct((chips, own + 8, rows), BF16),
             jax.ShapeDtypeStruct((fmw, rows), BF16),
         ),
-        place,
         hidden,
         w_down,
         tail,
         local,
         flops=2 * rows * fmw * w_down.shape[0],
         nbytes=4 * MIB,
-        in_specs=[pl.BlockSpec(memory_space=pltpu.SMEM)] + [vmem] * 4,
+        in_specs=[vmem] * 4,
         out_specs=(vmem,) * 3,
         scratch_shapes=[pltpu.VMEM((chips, 2, own + 8, rows), F32)],
+    )
+
+
+def join_kernel(mine_ref, both_ref, out_ref):
+    other = 1 - lax.axis_index("tp") % 2
+    out_ref[...] = (mine_ref[...] + both_ref[other].astype(F32)).astype(BF16)
+
+
+def join(mine, both):
+    vmem = pl.BlockSpec(memory_space=pltpu.VMEM)
+    return call(
+        join_kernel,
+        jax.ShapeDtypeStruct(mine.shape, BF16),
+        mine,
+        both,
+        flops=mine.size,
+        nbytes=mine.size * 8,
+        in_specs=[vmem, vmem],
+        out_specs=vmem,
     )
 
 
@@ -265,7 +280,6 @@
 def on_device(embeddings, projection, compress, w_up, w_down, output_norm_gain, out_grad):
     tp = lax.axis_size("tp")
     dp = lax.axis_size("dp")
-    me = lax.axis_index("tp")
     feat, fmw = w_up.shape[0], w_down.shape[1]
     own = fmw // tp
 
@@ -276,10 +290,10 @@
     hidden = jax.nn.gelu(pre * (1.0 / NORMED_SCALE), approximate=True).astype(BF16)
     tail = got[:, :fmw].astype(BF16)
 
-    place = jnp.stack([me % 2, me // 2]).astype(jnp.int32)
-    mine, theirs, gg_all = down(place, hidden, w_down, tail, local, own)
-    swap = [(i, i ^ 1) for i in range(tp)]
-    chip_sum = (mine + lax.ppermute(theirs, "tp", swap).astype(F32)).astype(BF16)
+    mine, theirs, gg_all = down(hidden, w_down, tail, local, own)
+    pairs = [[i, i + 1] for i in range(0, tp, 2)]
+    both = lax.all_gather(theirs, "tp", axis=0, tiled=False, axis_index_groups=pairs)
+    chip_sum = join(mine, both)
     same_core = [list(range(c, tp, 2)) for c in range(2)]
     arrived = lax.all_to_all(chip_sum, "tp", 0, 0, tiled=True, axis_index_groups=same_core)
 

time: 110 us -> 106 us (0.964)
  blocking collectives: 94.5 us -> 96.8 us
  starting transfers between devices: 2.28 us -> 0 us
  waiting for transfers between devices: 1.26 us -> 0 us
    all_gather x0 -> x1, blocking collectives: none -> 2.3 us  [on_device(): lax.all_gather(theirs, 'tp', axis=0, tiled=False, axis_index_groups=pairs)]
    ppermute x1 -> x0, starting transfers between devices: 2.28 us -> none  [on_device(): lax.ppermute(theirs, 'tp', swap).astype(F32)]
    ppermute x1 -> x0, waiting for transfers between devices: 1.26 us -> none  [on_device(): lax.ppermute(theirs, 'tp', swap).astype(F32)]
    pallas_call x4 -> x5, Pallas kernels: 7.67 us -> 6.71 us  [call(): pl.pallas_call(kernel, out_shape=out_shape, compiler_params=pltpu.Compile...]
  transfers between devices with their start and end apart: 1 -> 0, of which waited for: 1 -> 0; matrix products, arithmetic and copies ran while one was open for 0% -> 0% of each run, Pallas kernels for 0% -> 0%
where the time goes in v4:
time: 106 us
  blocking collectives  96.8 us (91%)
  Pallas kernels  6.71 us (6%)
    all_gather x1, blocking collectives, on_device(): got = lax.all_gather(sent.astype(F16), 'tp', axis=0, tiled=True)  35.7 us
    all_to_all x1, blocking collectives, on_device(): parts = lax.all_to_all(grad.reshape(dp, -1, fmw), 'dp', 0, 0, tiled=True)  25.4 us
    all_to_all x1, blocking collectives, on_device(): lax.all_to_all(chip_sum, 'tp', 0, 0, tiled=True, axis_index_groups=same_c...  16.8 us
    all_gather x1, blocking collectives, on_device(): every = lax.all_gather(message, 'tp', axis=0, tiled=False)  16.6 us
    pallas_call x5, Pallas kernels, call(): pl.pallas_call(kernel, out_shape=out_shape, compiler_params=pltpu.Compile...  6.71 us
    all_gather x1, blocking collectives, on_device(): lax.all_gather(theirs, 'tp', axis=0, tiled=False, axis_index_groups=pairs)  2.3 us

profile of v4, /device:TPU:8, one launch (start us, length us, event | category | flops | bytes accessed | tf_op | source)
XLA Modules:
  0.0 106.1 jit_solution(4227069286330825299)
XLA Ops:
  0.6 0.0 copy-start
  0.6 4.4 %shard_map.86 = (bf16[24,4864]{1,0:T(8,128)(2,1)S(1)}, f32[24,768]{1,0:T(8,128)S(1)}, f32[96,384]{1,0:T(8,128)S(1)}) custom-call(bf16[24,192,256]{2,1,0:T(8,128)(2,1)} %refs_0_.1, bf16[16,256]{1,0:T(8,128)(2,1)} %bitcast.15, bf16[4,256]{1,0:T(4,128)(2,1)} %bitcast.16, bf16[96,384]{1,0:T(8,128)(2,1)} %bitcast.14, f32[1,96]{1,0:T(1,128)} %bitcast.12), custom_call_target="tpu_custom_call" | custom-call | flops 339738624 | bytes 2359296 | tf_op jit(solution)/shard_map/pallas_call | solution.py:15
  5.1 35.7 %all-gather.3 = f16[384,4864]{1,0:T(8,128)(2,1)S(1)} all-gather(f16[24,4864]{1,0:T(8,128)(2,1)S(1)} %convert_element_type.15), channel_id=1, replica_groups=mesh['dp'=32,'tp'=16] {'tp'}, dimensions={0}, use_global_device_ids=true | all-gather | bytes 3969024 | tf_op jit(solution)/shard_map/all_gather | solution.py:287
  40.8 0.1 slice_convert_fusion.4.tail_ref
  40.9 0.0 copy-done
  40.9 0.0 copy-start.1
  40.9 1.0 fusion.9.hidden_ref
  41.9 0.0 copy-start.2
  41.9 0.0 copy-done.1
  42.0 0.9 shard_map.87
  42.9 2.3 %all-gather = bf16[16,56,384]{2,1,0:T(8,128)(2,1)S(1)} all-gather(bf16[8,56,384]{2,1,0:T(8,128)(2,1)S(1)} %get-tuple-element.15), channel_id=2, replica_groups={{0,1},{2,3},{4,5},{6,7},{8,9},{10,11},{12,13},{14,15},{16,17},{18,19},{..., dimensions={0}, use_global_device_ids=true | all-gather | bytes 1032192 | tf_op jit(solution)/shard_map/all_gather | solution.py:295
  45.2 0.1 shard_map.88
  45.3 16.8 %all_to_all.10.arrived_ref = bf16[8,56,384]{2,1,0:T(8,128)(2,1)S(1)} all-to-all(bf16[8,56,384]{2,1,0:T(8,128)(2,1)S(1)} %shard_map.88), channel_id=1, replica_groups={{0,2,4,6,8,10,12,14},{1,3,5,7,9,11,13,15},{16,18,20,22,24,26,28,30},{17..., dimensions={0} | all-to-all | bytes 688128 | tf_op jit(solution)/shard_map/all_to_all | solution.py:298
  62.1 0.1 shard_map.89
  62.2 16.6 %all-gather.1 = bf16[896,384]{1,0:T(8,128)(2,1)S(1)} all-gather(bf16[56,384]{1,0:T(8,128)(2,1)S(1)} %get-tuple-element.17), channel_id=3, replica_groups=mesh['dp'=32,'tp'=16] {'tp'}, dimensions={0}, use_global_device_ids=true | all-gather | bytes 731136 | tf_op jit(solution)/shard_map/all_gather | solution.py:301
  78.8 0.0 copy-done.2
  78.8 1.2 %shard_map.90 = (bf16[256,768]{1,0:T(8,128)(2,1)S(1)}, bf16[96,384]{1,0:T(8,128)(2,1)}) custom-call(bf16[16,56,384]{2,1,0:T(8,128)(2,1)S(1)} %bitcast.9, bf16[768,384]{1,0:T(8,128)(2,1)S(1)} %get-tuple-element.18.gg_ref, bf16[384,256]{1,0:T(8,128)(2,1)S(1)} %fusion.9.hidden_ref, f32[104,384]{1,0:T(8,128)S(1)} %get-tuple-element.19.delta_ref, ...), custom_call_target="tpu_custom_call" | custom-call | flops 150994944 | bytes 3145728 | tf_op jit(solution)/shard_map/pallas_call | solution.py:15
  80.0 25.4 %all_to_all.11 = bf16[32,8,768]{2,1,0:T(8,128)(2,1)S(1)} all-to-all(bf16[32,8,768]{2,1,0:T(8,128)(2,1)S(1)} %bitcast.11), channel_id=1, replica_groups=mesh['dp'=32,'tp'=16] {'dp'}, dimensions={0} | all-to-all | bytes 786432 | tf_op jit(solution)/shard_map/all_to_all | solution.py:303
  105.4 0.7 convert_reduce_fusion
  (1 shorter events, 0.0 us)
Async XLA Ops:
  0.6 40.2 %copy-start = (bf16[4096,256]{1,0:T(8,128)(2,1)S(1)}, bf16[4096,256]{1,0:T(8,128)(2,1)}, u32[]{:S(2)}) copy-start(bf16[4096,256]{1,0:T(8,128)(2,1)} %param.10) | copy-start | bytes 6291460
  40.9 1.1 %copy-start.1 = (bf16[256,768]{1,0:T(8,128)(2,1)S(1)}, bf16[256,768]{1,0:T(8,128)(2,1)}, u32[]{:S(2)}) copy-start(bf16[256,768]{1,0:T(8,128)(2,1)} %w_ref.1) | copy-start | bytes 1179652
  41.9 36.9 %copy-start.2 = (f32[96]{0:T(128)S(1)}, f32[96]{0:T(128)}, u32[]{:S(2)}) copy-start(f32[96]{0:T(128)} %param.12) | copy-start | bytes 1156

commit v5 on v4

--- a/solution.py
+++ b/solution.py
@@ -39,11 +39,12 @@
             zip(sources[1:], (projection_ref, compress_ref, og_ref, gain_ref))
         )
     ]
+    bounds = ((0, samples // 4), (samples // 4, samples))
     chunks = [
         pltpu.make_async_copy(
-            sources[0].at[pl.ds(r * block, block)], x_ref.at[pl.ds(r * block, block)], sems.at[len(copies) + r]
+            sources[0].at[pl.ds(at, end - at)], x_ref.at[pl.ds(at, end - at)], sems.at[len(copies) + c]
         )
-        for r in range(steps)
+        for c, (at, end) in enumerate(bounds)
     ]
     for copy in copies[:2] + chunks + copies[2:]:
         copy.start()
@@ -54,14 +55,19 @@
     w[:rank] = projection_ref[...].astype(F32)
     w[rank : rank + nl] = compress_ref[...].astype(F32)
     start = own * rows // samples
+    for c, (at, end) in enumerate(bounds):
+        chunks[c].wait()
+        if c == 1:
+            for copy in copies[2:]:
+                copy.wait()
+        x = x_ref[at:end]
+        both = lax.dot_general(x.reshape(-1, fields), w[...].astype(BF16), NT, preferred_element_type=F32)
+        for n in range(end - at):
+            r, i = divmod(at + n, block)
+            turned = both[n * edim : (n + 1) * edim].T
+            lcb[r, :, i, :] = turned[rank : rank + nl]
+            inter[r, :, i, :] = jnp.dot(turned[:rank].astype(BF16), x[n], preferred_element_type=F32)
     for r in range(steps):
-        chunks[r].wait()
-        x = x_ref[r * block : (r + 1) * block]
-        both = lax.dot_general(x.reshape(block * edim, fields), w[...].astype(BF16), NT, preferred_element_type=F32)
-        for i in range(block):
-            turned = both[i * edim : (i + 1) * edim].T
-            lcb[r, :, i, :] = turned[rank : rank + nl]
-            inter[r, :, i, :] = jnp.dot(turned[:rank].astype(BF16), x[i], preferred_element_type=F32)
         at = slice(r * block, (r + 1) * block)
         lines = [inter[r, k] for k in range(rank)]
         mean = jnp.sum(sum(lines[1:], lines[0]), axis=1, keepdims=True) / (rank * fields)
@@ -74,8 +80,6 @@
         for j in range(nl):
             lcb_ref[at, j * edim : (j + 1) * edim] = lcb[r, j]
 
-    for copy in copies[2:]:
-        copy.wait()
     gg = og_ref[...].astype(F32) * column(gain_ref[...])
     gg_ref[...] = gg
     for k in range(own // 8):
@@ -230,7 +234,7 @@
     )
 
 
-def grad_kernel(every_ref, gg_ref, hidden_ref, delta_ref, gain_ref, grad_ref, block_ref, dmix):
+def grad_kernel(every_ref, gg_ref, hidden_ref, delta_ref, gain_ref, grad_ref, block_ref, dmix, block, sem):
     tp, padded, rows = every_ref.shape
     own = padded - 8
     width = 2 * own
@@ -246,6 +250,10 @@
     rstd = 1.0 / jnp.sqrt(var + 1e-05)
     first = sum(n[2:3] for n in numbers) / full
     second = sum(n[3:4] + s * n[2:3] for n, s in zip(numbers, shifts)) * rstd / full
+    shift = delta_ref[width : width + 1] - mean
+    block[...] = ((delta_ref[:width] + shift) * rstd * column(gain_ref[...])).astype(BF16)
+    copy = pltpu.make_async_copy(block, block_ref, sem)
+    copy.start()
     scale = rstd * second
     for t in range(tp):
         offset = first + shifts[t] * scale
@@ -254,8 +262,7 @@
     grad_ref[...] = lax.dot_general(
         hidden_ref[...], dmix[...], (((0,), (1,)), ((), ())), preferred_element_type=F32
     ).astype(BF16)
-    shift = delta_ref[width : width + 1] - mean
-    block_ref[...] = ((delta_ref[:width] + shift) * rstd * column(gain_ref[...])).astype(BF16)
+    copy.wait()
 
 
 def down_gradient(every, gg, hidden, delta, gain):
@@ -272,8 +279,12 @@
         flops=2 * rows * fmw * hidden.shape[1],
         nbytes=3 * MIB,
         in_specs=[pl.BlockSpec(memory_space=pltpu.VMEM)] * 5,
-        out_specs=(pl.BlockSpec(memory_space=pltpu.VMEM),) * 2,
-        scratch_shapes=[pltpu.VMEM((fmw, rows), BF16)],
+        out_specs=(pl.BlockSpec(memory_space=pltpu.VMEM), pl.BlockSpec(memory_space=pltpu.HBM)),
+        scratch_shapes=[
+            pltpu.VMEM((fmw, rows), BF16),
+            pltpu.VMEM((width, rows), BF16),
+            pltpu.SemaphoreType.DMA,
+        ],
     )
 
 

time: 106 us -> 105 us (level)
  no operation moved by 1% of the time
where the time goes in v5:
time: 105 us
  blocking collectives  96.8 us (92%)
  Pallas kernels  5.7 us (5%)
  matrix products  1.05 us (1%)
    all_gather x1, blocking collectives, on_device(): got = lax.all_gather(sent.astype(F16), 'tp', axis=0, tiled=True)  35.7 us
    all_to_all x1, blocking collectives, on_device(): parts = lax.all_to_all(grad.reshape(dp, -1, fmw), 'dp', 0, 0, tiled=True)  25.4 us
    all_to_all x1, blocking collectives, on_device(): lax.all_to_all(chip_sum, 'tp', 0, 0, tiled=True, axis_index_groups=same_c...  16.8 us
    all_gather x1, blocking collectives, on_device(): every = lax.all_gather(message, 'tp', axis=0, tiled=False)  16.6 us
    pallas_call x5, Pallas kernels, call(): pl.pallas_call(kernel, out_shape=out_shape, compiler_params=pltpu.Compile...  5.7 us
    all_gather x1, blocking collectives, on_device(): lax.all_gather(theirs, 'tp', axis=0, tiled=False, axis_index_groups=pairs)  2.3 us

profile of v5, /device:TPU:8, one launch (start us, length us, event | category | flops | bytes accessed | tf_op | source)
XLA Modules:
  0.0 105.1 jit_solution(9971293690183561762)
XLA Ops:
  0.6 0.0 copy-start
  0.6 3.3 %shard_map.86 = (bf16[24,4864]{1,0:T(8,128)(2,1)S(1)}, f32[24,768]{1,0:T(8,128)S(1)}, f32[96,384]{1,0:T(8,128)S(1)}) custom-call(bf16[24,192,256]{2,1,0:T(8,128)(2,1)} %refs_0_.1, bf16[16,256]{1,0:T(8,128)(2,1)} %bitcast.15, bf16[4,256]{1,0:T(4,128)(2,1)} %bitcast.16, bf16[96,384]{1,0:T(8,128)(2,1)} %bitcast.14, f32[1,96]{1,0:T(1,128)} %bitcast.12), custom_call_target="tpu_custom_call" | custom-call | flops 339738624 | bytes 2359296 | tf_op jit(solution)/shard_map/pallas_call | solution.py:15
  4.1 35.7 %all-gather.3 = f16[384,4864]{1,0:T(8,128)(2,1)S(1)} all-gather(f16[24,4864]{1,0:T(8,128)(2,1)S(1)} %convert_element_type.15), channel_id=1, replica_groups=mesh['dp'=32,'tp'=16] {'tp'}, dimensions={0}, use_global_device_ids=true | all-gather | bytes 3969024 | tf_op jit(solution)/shard_map/all_gather | solution.py:298
  39.8 0.1 slice_convert_fusion.4.tail_ref
  39.8 0.0 copy-done
  39.8 0.0 copy-start.1
  39.9 1.0 fusion.9.hidden_ref
  40.9 0.0 copy-start.2
  40.9 0.0 copy-done.1
  40.9 0.9 shard_map.87
  41.8 2.3 %all-gather = bf16[16,56,384]{2,1,0:T(8,128)(2,1)S(1)} all-gather(bf16[8,56,384]{2,1,0:T(8,128)(2,1)S(1)} %get-tuple-element.15), channel_id=2, replica_groups={{0,1},{2,3},{4,5},{6,7},{8,9},{10,11},{12,13},{14,15},{16,17},{18,19},{..., dimensions={0}, use_global_device_ids=true | all-gather | bytes 1032192 | tf_op jit(solution)/shard_map/all_gather | solution.py:306
  44.1 0.1 shard_map.88
  44.2 16.8 %all_to_all.10.arrived_ref = bf16[8,56,384]{2,1,0:T(8,128)(2,1)S(1)} all-to-all(bf16[8,56,384]{2,1,0:T(8,128)(2,1)S(1)} %shard_map.88), channel_id=1, replica_groups={{0,2,4,6,8,10,12,14},{1,3,5,7,9,11,13,15},{16,18,20,22,24,26,28,30},{17..., dimensions={0} | all-to-all | bytes 688128 | tf_op jit(solution)/shard_map/all_to_all | solution.py:309
  61.1 0.1 shard_map.89
  61.2 16.6 %all-gather.1 = bf16[896,384]{1,0:T(8,128)(2,1)S(1)} all-gather(bf16[56,384]{1,0:T(8,128)(2,1)S(1)} %get-tuple-element.17), channel_id=3, replica_groups=mesh['dp'=32,'tp'=16] {'tp'}, dimensions={0}, use_global_device_ids=true | all-gather | bytes 731136 | tf_op jit(solution)/shard_map/all_gather | solution.py:312
  77.8 0.0 copy-done.2
  77.8 1.2 %shard_map.90 = (bf16[256,768]{1,0:T(8,128)(2,1)S(1)}, bf16[96,384]{1,0:T(8,128)(2,1)}) custom-call(bf16[16,56,384]{2,1,0:T(8,128)(2,1)S(1)} %bitcast.9, bf16[768,384]{1,0:T(8,128)(2,1)S(1)} %get-tuple-element.18.gg_ref, bf16[384,256]{1,0:T(8,128)(2,1)S(1)} %fusion.9.hidden_ref, f32[104,384]{1,0:T(8,128)S(1)} %get-tuple-element.19.delta_ref, ...), custom_call_target="tpu_custom_call" | custom-call | flops 150994944 | bytes 3145728 | tf_op jit(solution)/shard_map/pallas_call | solution.py:15
  79.0 25.4 %all_to_all.11 = bf16[32,8,768]{2,1,0:T(8,128)(2,1)S(1)} all-to-all(bf16[32,8,768]{2,1,0:T(8,128)(2,1)S(1)} %bitcast.11), channel_id=1, replica_groups=mesh['dp'=32,'tp'=16] {'dp'}, dimensions={0} | all-to-all | bytes 786432 | tf_op jit(solution)/shard_map/all_to_all | solution.py:314
  104.4 0.7 convert_reduce_fusion
  (1 shorter events, 0.0 us)
Async XLA Ops:
  0.6 39.2 %copy-start = (bf16[4096,256]{1,0:T(8,128)(2,1)S(1)}, bf16[4096,256]{1,0:T(8,128)(2,1)}, u32[]{:S(2)}) copy-start(bf16[4096,256]{1,0:T(8,128)(2,1)} %param.10) | copy-start | bytes 6291460
  39.8 1.1 %copy-start.1 = (bf16[256,768]{1,0:T(8,128)(2,1)S(1)}, bf16[256,768]{1,0:T(8,128)(2,1)}, u32[]{:S(2)}) copy-start(bf16[256,768]{1,0:T(8,128)(2,1)} %w_ref.1) | copy-start | bytes 1179652
  40.9 36.9 %copy-start.2 = (f32[96]{0:T(128)S(1)}, f32[96]{0:T(128)}, u32[]{:S(2)}) copy-start(f32[96]{0:T(128)} %param.12) | copy-start | bytes 1156
